TPU v7x, 32 devices: a whole 2x2x4 slice. The times are simulated.
32 devices in a mesh: row: 4 (over y, x), col: 8 (over z, core).
Axes of the slice: x: 2, y: 2, z: 4, core: 2. Of those that a mesh axis runs over, the one named last changes fastest.
Arguments:
- out_grad: bfloat16 [512, 8192], P('col', 'row'), may hold values from -6 to 6
- hidden: bfloat16 [512, 28672], P('row', 'col'), may hold values from -0.12988281 to 0.12988281
- weight: bfloat16 [28672, 8192], P('col', 'row'), may hold values from -0.03125 to 0.03125
Outputs:
- token_grad: bfloat16 [512, 28672], P('row', 'col')
- weight_grad: bfloat16 [28672, 8192], P('col', 'row')
All inputs are finite; a program needn't handle non-finite values.
Results may differ from a plain program's by a relative error of at most 0.001.
Values may be sent and summed in bfloat16 or wider, within the bound.
No kernel may reach another device: no remote copies, remote signals or barrier semaphores. Data moves between devices by JAX's collectives and lax.ppermute only.
A program may use at most 192 MiB of HBM per device.

v0:
```python
import jax
import jax.numpy as jnp
from jax import lax
from jax.sharding import PartitionSpec as P


def on_device(out_grad, hidden, weight):
    gathered = lax.all_gather(out_grad, "col", axis=0, tiled=True)
    cotangent = gathered
    weight_sum = lax.dot_general(
        lax.all_gather(hidden, "row", axis=0, tiled=True),
        cotangent,
        (((0,), (0,)), ((), ())),
        preferred_element_type=jnp.float32,
    )
    weight_grad = weight_sum.astype(jnp.bfloat16)
    own_full = lax.all_to_all(gathered, "row", split_axis=0, concat_axis=1, tiled=True)
    cotangent = own_full
    token_sum = lax.dot_general(
        cotangent,
        lax.all_gather(weight, "row", axis=1, tiled=True),
        (((1,), (1,)), ((), ())),
        preferred_element_type=jnp.float32,
    )
    return (token_sum.astype(jnp.bfloat16), weight_grad)


def solution(mesh):
    return jax.shard_map(
        on_device,
        mesh=mesh,
        in_specs=(P("col", "row"), P("row", "col"), P("col", "row")),
        out_specs=(P("row", "col"), P("col", "row")),
        check_vma=False,
    )
```

profile of v0, /device:TPU:0, one launch (start us, length us, event | category | flops | bytes accessed | tf_op | source)
XLA Modules:
  0.0 649.6 jit_solution(18092122016012289057)
XLA Ops:
  7.2 0.0 all-gather.4.cloned.1.call-start
  7.2 0.7 all-gather.4.cloned.1.call-update
  7.9 0.0 all-gather.8.cloned.1.call-start
  7.9 0.7 all-gather.8.cloned.1.call-update
  8.6 0.0 all-gather.6.cloned.1.call-start
  8.7 0.7 all-gather.6.cloned.1.call-update
  9.4 32.1 %all-gather.4.cloned.1.call-done = bf16[512,2048]{1,0:T(8,128)(2,1)} async-done(((bf16[64,2048]{1,0:T(8,128)(2,1)}), bf16[512,2048]{1,0:T(8,128)(2,1)}) %all-gather.4.cloned.1.call-update) | async-done | bytes 2097168 | tf_op jit(solution)/shard_map/all_gather | solution.py:8
  41.4 40.4 %all_to_all.19 = bf16[4,128,2048]{2,1,0:T(8,128)(2,1)} all-to-all(bf16[4,128,2048]{2,1,0:T(8,128)(2,1)} %bitcast.9), channel_id=1, replica_groups=mesh['row'=4,'col'=8] {'row'}, dimensions={0} | all-to-all | bytes 4194304 | tf_op jit(solution)/shard_map/all_to_all | solution.py:17
  81.8 3.0 copy.5
  84.8 22.6 %all-gather.8.cloned.1.call-done = bf16[512,3584]{1,0:T(8,128)(2,1)} async-done(((bf16[128,3584]{1,0:T(8,128)(2,1)}), bf16[512,3584]{1,0:T(8,128)(2,1)}) %all-gather.8.cloned.1.call-update) | async-done | bytes 3670032 | tf_op jit(solution)/shard_map/all_gather | solution.py:11
  107.4 15.9 %convolution_convert_fusion = bf16[3584,2048]{1,0:T(8,128)(2,1)} fusion(bf16[512,3584]{1,0:T(8,128)(2,1)} %all-gather.8.cloned.1.call-done, bf16[512,2048]{1,0:T(8,128)(2,1)} %all-gather.4.cloned.1.call-done), kind=kOutput, calls=%fused_computation | convolution fusion | flops 7523532800 | bytes 20447232 | tf_op jit(solution)/shard_map/dot_general | solution.py:10
  123.3 493.3 %all-gather.6.cloned.1.call-done = bf16[3584,8192]{1,0:T(8,128)(2,1)} async-done(((bf16[3584,2048]{1,0:T(8,128)(2,1)}), bf16[3584,8192]{1,0:T(8,128)(2,1)}) %all-gather.6.cloned.1.call-update) | async-done | bytes 58720272 | tf_op jit(solution)/shard_map/all_gather | solution.py:21
  616.6 26.5 %convolution_convert_fusion.1 = bf16[128,3584]{1,0:T(8,128)(2,1)} fusion(bf16[128,8192]{0,1:T(8,128)(2,1)S(1)} %bitcast.7, bf16[3584,8192]{1,0:T(8,128)(2,1)} %all-gather.6.cloned.1.call-done), kind=kOutput, calls=%fused_computation.1 | convolution fusion | flops 7516651520 | bytes 61734912 | tf_op jit(solution)/shard_map/dot_general | solution.py:19
Async XLA Ops:
  7.2 34.3 %all-gather.4.cloned.1.call-start = ((), (), s32[]{:S(2)}) async-start(), calls=%async_computation.1 | async-start | bytes 2359296 | tf_op jit(solution)/shard_map/all_gather | solution.py:8
  7.9 99.5 %all-gather.8.cloned.1.call-start = ((), (), s32[]{:S(2)}) async-start(), calls=%async_computation.3 | async-start | bytes 4587520 | tf_op jit(solution)/shard_map/all_gather | solution.py:11
  8.6 607.9 %all-gather.6.cloned.1.call-start = ((), (), s32[]{:S(2)}) async-start(), calls=%async_computation.2 | async-start | bytes 73400320 | tf_op jit(solution)/shard_map/all_gather | solution.py:21
Sparse Core Ops, SparseCore 0:
  9.6 31.7 all-gather.3
  43.3 64.0 all-gather.7
  109.3 507.2 all-gather.5
where the time goes:
time: 650 us
  waiting for transfers between devices  550 us (85%)
  matrix products  42.4 us (7%)
  blocking collectives  40.4 us (6%)
  between operations  13.7 us (2%)
    all_gather x1, waiting for transfers between devices, on_device(): lax.all_gather(weight, 'row', axis=1, tiled=True)  493 us
    all_to_all x1, blocking collectives, on_device(): lax.all_to_all(gathered, 'row', split_axis=0, concat_axis=1, tiled=True)  40.4 us
    all_gather x1, waiting for transfers between devices, on_device(): gathered = lax.all_gather(out_grad, 'col', axis=0, tiled=True)  32.1 us
    dot_general x1, matrix products, on_device(): lax.dot_general(cotangent, lax.all_gather(weight, 'row', axis=1, tiled=Tr...  26.5 us
    all_gather x1, waiting for transfers between devices, on_device(): lax.all_gather(hidden, 'row', axis=0, tiled=True)  22.6 us
    dot_general x1, matrix products, on_device(): lax.dot_general(lax.all_gather(hidden, 'row', axis=0, tiled=True), cotang...  15.9 us
  transfers between devices with their start and end apart: 3, of which 3 were waited for; matrix products, arithmetic and copies ran while one was open for 3% of the time, Pallas kernels for 0%

commit v1 on v0

v1 whole, which is shorter than its diff:
```python
import functools

import jax
import jax.numpy as jnp
from jax import lax
from jax.experimental import pallas as pl
from jax.experimental.pallas import tpu as pltpu
from jax.sharding import PartitionSpec as P

CORES = 2
SPAN = 120.0
SCALE_ROWS = 16
VMEM = 56 * 1024 * 1024


def grid_of(n):
    ny = int(n**0.5)
    while n % ny:
        ny -= 1
    return ny, n // ny


def encode(block):
    top = jnp.max(jnp.abs(block), axis=0, keepdims=True)
    scale = jnp.maximum(top * 1.0078125, 1e-36).astype(jnp.bfloat16)
    level = jnp.abs(block) * (2 * SPAN / scale.astype(jnp.float32)) - SPAN
    size = jnp.exp2(level)
    return jnp.where(block < 0, -size, size).astype(jnp.bfloat16), scale


def decode(code, scale):
    value = code.astype(jnp.float32)
    size = (jnp.log2(jnp.abs(value)) + SPAN) * (scale.astype(jnp.float32)[:1] * (0.5 / SPAN))
    return jnp.where(value < 0, -size, size)


def store_message(ref, block):
    rows = block.shape[0]
    code, scale = encode(block)
    ref[:rows, :] = code
    ref[rows:, :] = jnp.broadcast_to(scale, (SCALE_ROWS, block.shape[1]))


class Plan:
    def __init__(self, mesh):
        self.n, self.m = mesh.shape["row"], mesh.shape["col"]
        self.ny, self.nx = grid_of(self.n)
        self.nz = self.m // CORES

    def place(self):
        row, col = lax.axis_index("row"), lax.axis_index("col")
        return row // self.nx, row % self.nx, col // CORES, col % CORES

    def send_row(self, array, dy, dx):
        ny, nx = self.ny, self.nx
        pairs = [(y * nx + x, (y + dy) % ny * nx + (x + dx) % nx) for y in range(ny) for x in range(nx)]
        return lax.ppermute(array, "row", pairs)

    def peer_z(self, z, d):
        return z ^ d if self.nz & (self.nz - 1) == 0 else (z + d) % self.nz

    def from_z(self, z, d):
        return z ^ d if self.nz & (self.nz - 1) == 0 else (z + self.nz - d) % self.nz

    def send_z(self, array, d):
        pairs = [(z * CORES + c, self.peer_z(z, d) * CORES + c) for z in range(self.nz) for c in range(CORES)]
        return lax.ppermute(array, "col", pairs)

    def swap(self, array, d):
        pairs = [(z * CORES + c, z * CORES + (c + d) % CORES) for z in range(self.nz) for c in range(CORES)]
        return lax.ppermute(array, "col", pairs)

    def load_tokens(self, pieces, held, sems, x_major):
        y, x, z, core = self.place()
        rows = pieces[0].shape[0]
        per = self.m // self.n
        copies = []
        for at in range(len(pieces)):
            d, c = at // CORES, at % CORES
            origin = self.from_z(z, d) * CORES + lax.rem(core + CORES - c, CORES)
            owner = origin // per
            dy = lax.rem(owner // self.nx + self.ny - y, self.ny)
            dx = lax.rem(owner % self.nx + self.nx - x, self.nx)
            slot = dx * self.ny + dy if x_major else dy * self.nx + dx
            start = pl.multiple_of((slot * per + origin % per) * rows, rows)
            copies.append(pltpu.make_async_copy(pieces[at], held.at[pl.ds(start, rows), :], sems.at[at]))
        for copy in copies:
            copy.start()
        for copy in copies:
            copy.wait()

    def token_part(self, pieces, weight, first, width, tile, x_first):
        count, (rows, depth) = len(pieces), pieces[0].shape
        tokens = count * rows
        own = tokens // self.n
        peers, blocks = (self.nx, self.ny) if x_first else (self.ny, self.nx)
        group = blocks * own

        def kernel(*refs):
            parts, weight_ref = refs[:count], refs[count]
            messages, keep = refs[count + 1 : count + peers], refs[count + peers]
            held, sems = refs[-2:]

            @pl.when(pl.program_id(0) == 0)
            def _():
                self.load_tokens(parts, held, sems, x_first)

            total = lax.dot_general(
                held[...], weight_ref[...], (((1,), (1,)), ((), ())), preferred_element_type=jnp.float32
            )
            keep[...] = total[:group]
            for peer in range(1, peers):
                store_message(messages[peer - 1], total[peer * group : (peer + 1) * group])

        message = jax.ShapeDtypeStruct((group + SCALE_ROWS, width), jnp.bfloat16)
        out = pl.pallas_call(
            kernel,
            grid=(width // tile,),
            in_specs=[pl.BlockSpec(memory_space=pl.ANY)] * count
            + [pl.BlockSpec((tile, depth), lambda i: (first // tile + i, 0))],
            out_specs=[pl.BlockSpec((group + SCALE_ROWS, tile), lambda i: (0, i))] * (peers - 1)
            + [pl.BlockSpec((group, tile), lambda i: (0, i))],
            out_shape=[message] * (peers - 1) + [jax.ShapeDtypeStruct((group, width), jnp.float32)],
            scratch_shapes=[pltpu.VMEM((tokens, depth), jnp.bfloat16), pltpu.SemaphoreType.DMA((count,))],
            compiler_params=pltpu.CompilerParams(vmem_limit_bytes=VMEM),
            cost_estimate=pl.CostEstimate(
                flops=2 * tokens * depth * width,
                bytes_accessed=2 * (tokens + width) * depth + 4 * tokens * width,
                transcendentals=tokens * width,
            ),
            name="token_part",
        )(*pieces, weight)
        return out[:-1], out[-1]

    def combine(self, got, keep, blocks):
        count, width = len(got), keep.shape[1]
        group = keep.shape[0]
        own = group // blocks

        def kernel(*refs):
            messages, keep_ref, outs = refs[:count], refs[count], refs[count + 1 :]
            for block in range(1, blocks):
                rows = slice(block * own, (block + 1) * own)
                total = keep_ref[rows, :]
                for message in messages:
                    total = total + decode(message[rows, :], message[group:, :])
                store_message(outs[block - 1], total)

        tile = width
        return pl.pallas_call(
            kernel,
            grid=(width // tile,),
            in_specs=[pl.BlockSpec((group + SCALE_ROWS, tile), lambda i: (0, i))] * count
            + [pl.BlockSpec((group, tile), lambda i: (0, i))],
            out_specs=[pl.BlockSpec((own + SCALE_ROWS, tile), lambda i: (0, i))] * (blocks - 1),
            out_shape=[jax.ShapeDtypeStruct((own + SCALE_ROWS, width), jnp.bfloat16)] * (blocks - 1),
            compiler_params=pltpu.CompilerParams(vmem_limit_bytes=VMEM),
            cost_estimate=pl.CostEstimate(
                flops=20 * group * width, bytes_accessed=8 * group * width, transcendentals=2 * group * width
            ),
            name="combine",
        )(*got, keep)

    def finish(self, chunks, own):
        total_width = sum(chunk[1] for chunk in chunks)
        operands, in_specs = [], []
        for first, width, keep, got, late in chunks:
            group = keep.shape[0]
            operands.append(keep)
            in_specs.append(pl.BlockSpec((own, width), lambda i: (0, 0)))
            for array in got:
                operands += [array, array]
                in_specs.append(pl.BlockSpec((own, width), lambda i: (0, 0)))
                in_specs.append(pl.BlockSpec((SCALE_ROWS, width), lambda i, at=group // SCALE_ROWS: (at, 0)))
            for array in late:
                operands.append(array)
                in_specs.append(pl.BlockSpec((own + SCALE_ROWS, width), lambda i: (0, 0)))

        def kernel(*refs):
            out, at = refs[-1], 0
            for first, width, keep, got, late in chunks:
                total = refs[at][...]
                at += 1
                for _ in got:
                    total = total + decode(refs[at][...], refs[at + 1][...])
                    at += 2
                for _ in late:
                    total = total + decode(refs[at][:own, :], refs[at][own:, :])
                    at += 1
                out[:, first : first + width] = total.astype(jnp.bfloat16)

        return pl.pallas_call(
            kernel,
            grid=(1,),
            in_specs=in_specs,
            out_specs=pl.BlockSpec((own, total_width), lambda i: (0, 0)),
            out_shape=jax.ShapeDtypeStruct((own, total_width), jnp.bfloat16),
            compiler_params=pltpu.CompilerParams(vmem_limit_bytes=VMEM),
            cost_estimate=pl.CostEstimate(
                flops=30 * own * total_width, bytes_accessed=12 * own * total_width, transcendentals=2 * own * total_width
            ),
            name="finish",
        )(*operands)

    def weight_part(self, pieces, blocks, tile):
        count, (rows, width) = len(pieces), pieces[0].shape
        tokens = count * rows
        units = blocks[0].shape[1]
        many = len(blocks)

        def kernel(*refs):
            parts, hidden = refs[:count], refs[count : count + many]
            out, held, sems = refs[count + many :]

            @pl.when(pl.program_id(0) == 0)
            def _():
                self.load_tokens(parts, held, sems, False)

            full = jnp.concatenate([ref[...] for ref in hidden], axis=0)
            out[...] = lax.dot_general(
                full, held[...], (((0,), (0,)), ((), ())), preferred_element_type=jnp.float32
            ).astype(jnp.bfloat16)

        return pl.pallas_call(
            kernel,
            grid=(units // tile,),
            in_specs=[pl.BlockSpec(memory_space=pl.ANY)] * count
            + [pl.BlockSpec((block.shape[0], tile), lambda i: (0, i)) for block in blocks],
            out_specs=pl.BlockSpec((tile, width), lambda i: (i, 0)),
            out_shape=jax.ShapeDtypeStruct((units, width), jnp.bfloat16),
            scratch_shapes=[pltpu.VMEM((tokens, width), jnp.bfloat16), pltpu.SemaphoreType.DMA((count,))],
            compiler_params=pltpu.CompilerParams(vmem_limit_bytes=VMEM),
            cost_estimate=pl.CostEstimate(
                flops=2 * tokens * units * width,
                bytes_accessed=2 * (tokens * (units + width) + units * width),
                transcendentals=0,
            ),
            name="weight_part",
        )(*pieces, *blocks)


def split(total, tile):
    tiles = total // tile
    parts = min(4, tiles)
    sizes = [tiles // parts + (at < tiles % parts) for at in range(parts)]
    chunks, first = [], 0
    for at, size in enumerate(sizes):
        chunks.append((first * tile, size * tile, at % 2 == 0))
        first += size
    return chunks


def on_device(plan, out_grad, hidden, weight):
    ny, nx = plan.ny, plan.nx
    pieces = []
    for d in range(plan.nz):
        piece = plan.send_z(out_grad, d) if d else out_grad
        pieces += [piece] + [plan.swap(piece, c) for c in range(1, CORES)]

    own = hidden.shape[0]
    half = own // 2
    at_x = [hidden] + [plan.send_row(hidden, 0, dx) for dx in range(1, nx)]
    at_y = [hidden] + [plan.send_row(hidden, dy, 0) for dy in range(1, ny)]

    def block_of(dy, dx):
        if dy == 0:
            return [at_x[dx]]
        if dx == 0:
            return [at_y[dy]]
        return [plan.send_row(at_x[dx][:half], dy, 0), plan.send_row(at_y[dy][half:], 0, dx)]

    blocks = []
    for sy in range(ny):
        for sx in range(nx):
            blocks += block_of((ny - sy) % ny, (nx - sx) % nx)

    units = hidden.shape[1]
    tile = 256 if units % 256 == 0 else 128
    parts = []
    for first, width, x_first in split(units, tile):
        messages, keep = plan.token_part(pieces, weight, first, width, tile, x_first)
        got = [plan.send_row(msg, 0, d + 1) if x_first else plan.send_row(msg, d + 1, 0) for d, msg in enumerate(messages)]
        parts.append((first, width, x_first, keep, got))

    weight_grad = plan.weight_part(pieces, blocks, tile)

    chunks = []
    for first, width, x_first, keep, got in parts:
        onward = plan.combine(got, keep, ny if x_first else nx)
        late = [plan.send_row(msg, d + 1, 0) if x_first else plan.send_row(msg, 0, d + 1) for d, msg in enumerate(onward)]
        chunks.append((first, width, keep, got, late))
    return plan.finish(chunks, own), weight_grad


def solution(mesh):
    return jax.shard_map(
        functools.partial(on_device, Plan(mesh)),
        mesh=mesh,
        in_specs=(P("col", "row"), P("row", "col"), P("col", "row")),
        out_specs=(P("row", "col"), P("col", "row")),
        check_vma=False,
    )
```

time: 650 us -> 126 us (0.19)
  waiting for transfers between devices: 550 us -> 39.2 us
  Pallas kernels: 0 us -> 58.7 us
  matrix products: 42.4 us -> 0 us
  blocking collectives: 40.4 us -> 0 us
  starting transfers between devices: 0.11 us -> 21.7 us
  between operations: 13.7 us -> 0.83 us
    all_gather x3 -> x0, waiting for transfers between devices: 548 us -> none  [the longest x1 493 us: on_device(): lax.all_gather(weight, 'row', axis=1, tiled=True)]
    pallas_call x0 -> x10, Pallas kernels: none -> 58.7 us  [the longest x4 27.9 us: token_part(): pl.pallas_call(kernel, grid=(width // tile,), in_specs=[pl.BlockSpec(memo...]
    dot_general x2 -> x0, matrix products: 42.4 us -> none  [the longest x1 26.5 us: on_device(): lax.dot_general(cotangent, lax.all_gather(weight, 'row', axis=1, tiled=Tr...]
    all_to_all x1 -> x0, blocking collectives: 40.4 us -> none  [on_device(): lax.all_to_all(gathered, 'row', split_axis=0, concat_axis=1, tiled=True)]
    ppermute x0 -> x19, waiting for transfers between devices: none -> 39.2 us  [the longest x12 19 us: send_row(): return lax.ppermute(array, 'row', pairs)]
    ppermute x0 -> x19, starting transfers between devices: none -> 21.7 us  [the longest x12 15.4 us: send_row(): return lax.ppermute(array, 'row', pairs)]
  transfers between devices with their start and end apart: 3 -> 19, of which waited for: 3 -> 6; matrix products, arithmetic and copies ran while one was open for 3% -> 0% of each run, Pallas kernels for 0% -> 44%
where the time goes in v1:
time: 126 us; the launch traced here: 124 us
  Pallas kernels  58.7 us (47%)
  waiting for transfers between devices  39.2 us (31%)
  starting transfers between devices  21.7 us (17%)
  local copies, waits for them, and re-layouts  3.54 us (3%)
    pallas_call x4, Pallas kernels, token_part(): pl.pallas_call(kernel, grid=(width // tile,), in_specs=[pl.BlockSpec(memo...  27.9 us
    ppermute x12, waiting for transfers between devices, send_row(): return lax.ppermute(array, 'row', pairs)  19 us
    ppermute x3, waiting for transfers between devices, send_z(): return lax.ppermute(array, 'col', pairs)  18.5 us
    pallas_call x1, Pallas kernels, weight_part(): pl.pallas_call(kernel, grid=(units // tile,), in_specs=[pl.BlockSpec(memo...  17 us
    ppermute x12, starting transfers between devices, send_row(): return lax.ppermute(array, 'row', pairs)  15.4 us
    pallas_call x4, Pallas kernels, combine(): pl.pallas_call(kernel, grid=(width // tile,), in_specs=[pl.BlockSpec((gro...  9.63 us
    ppermute x3, starting transfers between devices, send_z(): return lax.ppermute(array, 'col', pairs)  5.76 us
    pallas_call x1, Pallas kernels, finish(): pl.pallas_call(kernel, grid=(1,), in_specs=in_specs, out_specs=pl.BlockSp...  4.09 us
  transfers between devices with their start and end apart: 19, of which 6 were waited for; matrix products, arithmetic and copies ran while one was open for 0% of the time, Pallas kernels for 44%

profile of v1, /device:TPU:0, one launch (start us, length us, event | category | flops | bytes accessed | tf_op | source)
XLA Modules:
  0.0 124.0 jit_solution(9771629411457821620)
XLA Ops:
  0.6 5.1 %collective-permute-start.5 = (bf16[64,2048]{1,0:T(8,128)(2,1)}, bf16[64,2048]{1,0:T(8,128)(2,1)S(1)}, u32[]{:S(2)}, u32[]{:S(2)}) collective-permute-start(bf16[64,2048]{1,0:T(8,128)(2,1)} %refs_0_.9), channel_id=1, source_target_pairs={{0,6},{1,7},{2,4},{3,5},{4,2},{5,3},{6,0},{7,1},{8,14},{9,15},{10,... | collective-permute-start | bytes 786440 | tf_op jit(solution)/shard_map/ppermute | solution.py:67
  5.7 0.0 collective-permute-start.3
  5.7 0.6 collective-permute-start.1
  6.4 0.0 collective-permute-start
  6.4 1.6 %collective-permute-start.15 = (bf16[128,3584]{1,0:T(8,128)(2,1)}, bf16[128,3584]{1,0:T(8,128)(2,1)S(1)}, u32[]{:S(2)}, u32[]{:S(2)}) collective-permute-start(bf16[128,3584]{1,0:T(8,128)(2,1)} %refs_8_.9), channel_id=1, source_target_pairs={{0,8},{8,0},{16,24},{24,16},{1,9},{9,1},{17,25},{25,17},{2,10},{10... | collective-permute-start | bytes 2752520 | tf_op jit(solution)/shard_map/ppermute | solution.py:57
  8.0 5.2 %collective-permute-done.5.refs_6_ = bf16[64,2048]{1,0:T(8,128)(2,1)S(1)} collective-permute-done((bf16[64,2048]{1,0:T(8,128)(2,1)}, bf16[64,2048]{1,0:T(8,128)(2,1)S(1)}, u32[]{:S(2)}, u32[]{:S(2)}) %collective-permute-start.5) | collective-permute-done | bytes 262176 | tf_op jit(solution)/shard_map/ppermute | solution.py:67
  13.2 1.7 %collective-permute-start.16 = (bf16[128,3584]{1,0:T(8,128)(2,1)}, bf16[128,3584]{1,0:T(8,128)(2,1)S(1)}, u32[]{:S(2)}, u32[]{:S(2)}) collective-permute-start(bf16[128,3584]{1,0:T(8,128)(2,1)} %refs_8_.9), channel_id=1, source_target_pairs={{0,16},{8,24},{16,0},{24,8},{1,17},{9,25},{17,1},{25,9},{2,18},{10... | collective-permute-start | bytes 2752520 | tf_op jit(solution)/shard_map/ppermute | solution.py:57
  15.0 13.3 %collective-permute-done.3.refs_4_ = bf16[64,2048]{1,0:T(8,128)(2,1)S(1)} collective-permute-done((bf16[64,2048]{1,0:T(8,128)(2,1)}, bf16[64,2048]{1,0:T(8,128)(2,1)S(1)}, u32[]{:S(2)}, u32[]{:S(2)}) %collective-permute-start.3) | collective-permute-done | bytes 262176 | tf_op jit(solution)/shard_map/ppermute | solution.py:67
  28.3 0.0 collective-permute-start.6
  28.3 0.0 collective-permute-done.1.refs_2_
  28.3 0.0 copy-start.4
  28.3 0.5 collective-permute-start.4
  28.8 0.0 collective-permute-done.refs_1_
  28.8 0.1 collective-permute-start.2
  28.9 0.9 collective-permute-done.6.refs_7_
  29.8 0.4 collective-permute-done.4.refs_5_
  30.2 0.4 collective-permute-done.2.refs_3_
  30.6 0.0 copy-done.2
  30.6 0.0 copy-done.3
  30.6 0.0 copy-done.4
  30.6 0.0 copy-done.5
  30.6 0.0 copy-done.6
  30.6 0.3 copy-done.7
  30.9 0.7 copy-done.8
  31.6 6.5 %token_part.7 = (bf16[272,768]{1,0:T(8,128)(2,1)}, f32[256,768]{1,0:T(8,128)}) custom-call(bf16[64,2048]{1,0:T(8,128)(2,1)} %refs_0_.9, bf16[64,2048]{1,0:T(8,128)(2,1)} %copy-done.5, bf16[64,2048]{1,0:T(8,128)(2,1)} %copy-done.4, bf16[64,2048]{1,0:T(8,128)(2,1)} %copy-done.8, bf16[64,2048]{1,0:T(8,128)(2,1)} %copy-done.3, bf16[64,2048]{1,0:T(8,128)(2,1)} %copy-done.7, ...), custom_call_target="tpu_custom_call" | custom-call | flops 1610612736 | bytes 6815744 | tf_op jit(solution)/shard_map/token_part/pallas_call | solution.py:116
  38.1 1.6 %collective-permute-start.13 = (bf16[272,768]{1,0:T(8,128)(2,1)}, bf16[272,768]{1,0:T(8,128)(2,1)S(1)}, u32[]{:S(2)}, u32[]{:S(2)}) collective-permute-start(bf16[272,768]{1,0:T(8,128)(2,1)} %get-tuple-element.17), channel_id=1, source_target_pairs={{0,16},{8,24},{16,0},{24,8},{1,17},{9,25},{17,1},{25,9},{2,18},{10... | collective-permute-start | bytes 1253384 | tf_op jit(solution)/shard_map/ppermute | solution.py:57
  39.7 7.5 %token_part.5 = (bf16[272,1024]{1,0:T(8,128)(2,1)}, f32[256,1024]{1,0:T(8,128)}) custom-call(bf16[64,2048]{1,0:T(8,128)(2,1)} %refs_0_.9, bf16[64,2048]{1,0:T(8,128)(2,1)} %copy-done.5, bf16[64,2048]{1,0:T(8,128)(2,1)} %copy-done.4, bf16[64,2048]{1,0:T(8,128)(2,1)} %copy-done.8, bf16[64,2048]{1,0:T(8,128)(2,1)} %copy-done.3, bf16[64,2048]{1,0:T(8,128)(2,1)} %copy-done.7, ...), custom_call_target="tpu_custom_call" | custom-call | flops 2147483648 | bytes 8388608 | tf_op jit(solution)/shard_map/token_part/pallas_call | solution.py:116
  47.2 0.6 collective-permute-start.9
  47.7 7.4 %token_part.4 = (bf16[272,1024]{1,0:T(8,128)(2,1)}, f32[256,1024]{1,0:T(8,128)}) custom-call(bf16[64,2048]{1,0:T(8,128)(2,1)} %refs_0_.9, bf16[64,2048]{1,0:T(8,128)(2,1)} %copy-done.5, bf16[64,2048]{1,0:T(8,128)(2,1)} %copy-done.4, bf16[64,2048]{1,0:T(8,128)(2,1)} %copy-done.8, bf16[64,2048]{1,0:T(8,128)(2,1)} %copy-done.3, bf16[64,2048]{1,0:T(8,128)(2,1)} %copy-done.7, ...), custom_call_target="tpu_custom_call" | custom-call | flops 2147483648 | bytes 8388608 | tf_op jit(solution)/shard_map/token_part/pallas_call | solution.py:116
  55.2 1.6 %collective-permute-start.7 = (bf16[272,1024]{1,0:T(8,128)(2,1)}, bf16[272,1024]{1,0:T(8,128)(2,1)S(1)}, u32[]{:S(2)}, u32[]{:S(2)}) collective-permute-start(bf16[272,1024]{1,0:T(8,128)(2,1)} %get-tuple-element.11), channel_id=1, source_target_pairs={{0,8},{8,0},{16,24},{24,16},{1,9},{9,1},{17,25},{25,17},{2,10},{10... | collective-permute-start | bytes 1671176 | tf_op jit(solution)/shard_map/ppermute | solution.py:57
  56.7 0.0 collective-permute-done.15.refs_9_
  56.8 1.6 %collective-permute-start.17 = (bf16[64,3584]{1,0:T(8,128)(2,1)S(1)}, bf16[64,3584]{1,0:T(8,128)(2,1)S(1)}, u32[]{:S(2)}, u32[]{:S(2)}) collective-permute-start(bf16[64,3584]{1,0:T(8,128)(2,1)S(1)} %slice.8), channel_id=1, source_target_pairs={{0,16},{8,24},{16,0},{24,8},{1,17},{9,25},{17,1},{25,9},{2,18},{10... | collective-permute-start | bytes 1376264 | tf_op jit(solution)/shard_map/ppermute | solution.py:57
  58.4 0.0 collective-permute-done.16.refs_10_
  58.4 0.6 collective-permute-start.18
  59.0 6.5 %token_part.6 = (bf16[272,768]{1,0:T(8,128)(2,1)}, f32[256,768]{1,0:T(8,128)}) custom-call(bf16[64,2048]{1,0:T(8,128)(2,1)} %refs_0_.9, bf16[64,2048]{1,0:T(8,128)(2,1)} %copy-done.5, bf16[64,2048]{1,0:T(8,128)(2,1)} %copy-done.4, bf16[64,2048]{1,0:T(8,128)(2,1)} %copy-done.8, bf16[64,2048]{1,0:T(8,128)(2,1)} %copy-done.3, bf16[64,2048]{1,0:T(8,128)(2,1)} %copy-done.7, ...), custom_call_target="tpu_custom_call" | custom-call | flops 1610612736 | bytes 6815744 | tf_op jit(solution)/shard_map/token_part/pallas_call | solution.py:116
  65.5 0.0 collective-permute-done.13.refs_0_.refs_13_.refs_14_
  65.6 1.6 %collective-permute-start.11 = (bf16[272,768]{1,0:T(8,128)(2,1)}, bf16[272,768]{1,0:T(8,128)(2,1)S(1)}, u32[]{:S(2)}, u32[]{:S(2)}) collective-permute-start(bf16[272,768]{1,0:T(8,128)(2,1)} %get-tuple-element.15), channel_id=1, source_target_pairs={{0,8},{8,0},{16,24},{24,16},{1,9},{9,1},{17,25},{25,17},{2,10},{10... | collective-permute-start | bytes 1253384 | tf_op jit(solution)/shard_map/ppermute | solution.py:57
  67.1 2.3 %combine.7 = bf16[144,768]{1,0:T(8,128)(2,1)} custom-call(bf16[272,768]{1,0:T(8,128)(2,1)} %copy-done.9, f32[256,768]{1,0:T(8,128)} %get-tuple-element.16.refs_1_.refs_12_), custom_call_target="tpu_custom_call" | custom-call | flops 3932160 | bytes 1572864 | tf_op jit(solution)/shard_map/combine/pallas_call | solution.py:150
  69.4 19.0 %collective-permute-done.11.refs_0_.refs_9_.refs_10_ = bf16[272,768]{1,0:T(8,128)(2,1)S(1)} collective-permute-done((bf16[272,768]{1,0:T(8,128)(2,1)}, bf16[272,768]{1,0:T(8,128)(2,1)S(1)}, u32[]{:S(2)}, u32[]{:S(2)}) %collective-permute-start.11) | collective-permute-done | bytes 417824 | tf_op jit(solution)/shard_map/ppermute | solution.py:57
  88.4 1.5 %collective-permute-start.14 = (bf16[144,768]{1,0:T(8,128)(2,1)}, bf16[144,768]{1,0:T(8,128)(2,1)S(1)}, u32[]{:S(2)}, u32[]{:S(2)}) collective-permute-start(bf16[144,768]{1,0:T(8,128)(2,1)} %combine.7), channel_id=1, source_target_pairs={{0,8},{8,0},{16,24},{24,16},{1,9},{9,1},{17,25},{25,17},{2,10},{10... | collective-permute-start | bytes 663560 | tf_op jit(solution)/shard_map/ppermute | solution.py:57
  89.9 2.3 %combine.6 = bf16[144,768]{1,0:T(8,128)(2,1)} custom-call(bf16[272,768]{1,0:T(8,128)(2,1)} %copy-done.10, f32[256,768]{1,0:T(8,128)} %get-tuple-element.14.refs_1_.refs_8_), custom_call_target="tpu_custom_call" | custom-call | flops 3932160 | bytes 1572864 | tf_op jit(solution)/shard_map/combine/pallas_call | solution.py:150
  92.1 0.0 collective-permute-done.9.refs_0_.refs_5_.refs_6_
  92.1 1.5 %collective-permute-start.12 = (bf16[144,768]{1,0:T(8,128)(2,1)}, bf16[144,768]{1,0:T(8,128)(2,1)S(1)}, u32[]{:S(2)}, u32[]{:S(2)}) collective-permute-start(bf16[144,768]{1,0:T(8,128)(2,1)} %combine.6), channel_id=1, source_target_pairs={{0,16},{8,24},{16,0},{24,8},{1,17},{9,25},{17,1},{25,9},{2,18},{10... | collective-permute-start | bytes 663560 | tf_op jit(solution)/shard_map/ppermute | solution.py:57
  93.7 2.5 %combine.5 = bf16[144,1024]{1,0:T(8,128)(2,1)} custom-call(bf16[272,1024]{1,0:T(8,128)(2,1)} %copy-done, f32[256,1024]{1,0:T(8,128)} %get-tuple-element.12.refs_1_.refs_4_), custom_call_target="tpu_custom_call" | custom-call | flops 5242880 | bytes 2097152 | tf_op jit(solution)/shard_map/combine/pallas_call | solution.py:150
  96.2 0.0 collective-permute-done.7.refs_0_.refs_1_.refs_2_
  96.2 0.7 collective-permute-start.10
  97.0 0.1 copy-done.1
  97.0 2.6 %combine.4 = bf16[144,1024]{1,0:T(8,128)(2,1)} custom-call(bf16[272,1024]{1,0:T(8,128)(2,1)} %copy-done.1, f32[256,1024]{1,0:T(8,128)} %get-tuple-element.10.refs_1_.refs_0_), custom_call_target="tpu_custom_call" | custom-call | flops 5242880 | bytes 2097152 | tf_op jit(solution)/shard_map/combine/pallas_call | solution.py:150
  99.6 0.0 collective-permute-done.17.refs_11_
  99.6 0.8 collective-permute-start.8
  100.4 0.0 collective-permute-done.18.refs_12_
  100.4 0.0 copy-done.14
  100.4 0.8 copy-done.18
  101.2 17.0 %weight_part.1 = bf16[3584,2048]{1,0:T(8,128)(2,1)} custom-call(bf16[64,2048]{1,0:T(8,128)(2,1)} %refs_0_.9, bf16[64,2048]{1,0:T(8,128)(2,1)} %copy-done.5, bf16[64,2048]{1,0:T(8,128)(2,1)} %copy-done.4, bf16[64,2048]{1,0:T(8,128)(2,1)} %copy-done.8, bf16[64,2048]{1,0:T(8,128)(2,1)} %copy-done.3, bf16[64,2048]{1,0:T(8,128)(2,1)} %copy-done.7, ...), custom_call_target="tpu_custom_call" | custom-call | flops 7516192768 | bytes 20447232 | tf_op jit(solution)/shard_map/weight_part/pallas_call | solution.py:224
  118.2 0.0 collective-permute-done.14.refs_15_
  118.2 0.0 copy-start.15
  118.2 0.0 collective-permute-done.12.refs_11_
  118.2 0.0 collective-permute-done.10.refs_7_
  118.3 0.0 collective-permute-done.8.refs_3_
  118.3 0.6 copy-done.15
  118.9 0.1 copy-done.16
  119.0 0.1 copy-done.11
  119.1 0.7 copy-done.12
  119.9 4.1 %finish.1 = bf16[128,3584]{1,0:T(8,128)(2,1)} custom-call(f32[256,1024]{1,0:T(8,128)} %get-tuple-element.10.refs_1_.refs_0_, bf16[272,1024]{1,0:T(8,128)(2,1)} %copy-done.1, bf16[272,1024]{1,0:T(8,128)(2,1)} %copy-done.1, bf16[144,1024]{1,0:T(8,128)(2,1)} %copy-done.12, f32[256,1024]{1,0:T(8,128)} %get-tuple-element.12.refs_1_.refs_4_, ...), custom_call_target="tpu_custom_call" | custom-call | flops 13762560 | bytes 5505024 | tf_op jit(solution)/shard_map/finish/pallas_call | solution.py:192
  (24 shorter events, 0.1 us)
Async XLA Ops:
  0.6 12.6 %collective-permute-start.5 = (bf16[64,2048]{1,0:T(8,128)(2,1)}, bf16[64,2048]{1,0:T(8,128)(2,1)S(1)}, u32[]{:S(2)}, u32[]{:S(2)}) collective-permute-start(bf16[64,2048]{1,0:T(8,128)(2,1)} %refs_0_.9), channel_id=1, source_target_pairs={{0,6},{1,7},{2,4},{3,5},{4,2},{5,3},{6,0},{7,1},{8,14},{9,15},{10,... | collective-permute-start | bytes 786440 | tf_op jit(solution)/shard_map/ppermute | solution.py:67
  5.7 22.5 %collective-permute-start.3 = (bf16[64,2048]{1,0:T(8,128)(2,1)}, bf16[64,2048]{1,0:T(8,128)(2,1)S(1)}, u32[]{:S(2)}, u32[]{:S(2)}) collective-permute-start(bf16[64,2048]{1,0:T(8,128)(2,1)} %refs_0_.9), channel_id=1, source_target_pairs={{0,4},{1,5},{2,6},{3,7},{4,0},{5,1},{6,2},{7,3},{8,12},{9,13},{10,... | collective-permute-start | bytes 786440 | tf_op jit(solution)/shard_map/ppermute | solution.py:67
  5.7 22.5 %collective-permute-start.1 = (bf16[64,2048]{1,0:T(8,128)(2,1)}, bf16[64,2048]{1,0:T(8,128)(2,1)S(1)}, u32[]{:S(2)}, u32[]{:S(2)}) collective-permute-start(bf16[64,2048]{1,0:T(8,128)(2,1)} %refs_0_.9), channel_id=1, source_target_pairs={{0,2},{1,3},{2,0},{3,1},{4,6},{5,7},{6,4},{7,5},{8,10},{9,11},{10,... | collective-permute-start | bytes 786440 | tf_op jit(solution)/shard_map/ppermute | solution.py:67
  6.4 22.4 %collective-permute-start = (bf16[64,2048]{1,0:T(8,128)(2,1)}, bf16[64,2048]{1,0:T(8,128)(2,1)S(1)}, u32[]{:S(2)}, u32[]{:S(2)}) collective-permute-start(bf16[64,2048]{1,0:T(8,128)(2,1)} %refs_0_.9), channel_id=1, source_target_pairs={{0,1},{1,0},{2,3},{3,2},{4,5},{5,4},{6,7},{7,6},{8,9},{9,8},{10,11... | collective-permute-start | bytes 786440 | tf_op jit(solution)/shard_map/ppermute | solution.py:71
  6.4 50.4 %collective-permute-start.15 = (bf16[128,3584]{1,0:T(8,128)(2,1)}, bf16[128,3584]{1,0:T(8,128)(2,1)S(1)}, u32[]{:S(2)}, u32[]{:S(2)}) collective-permute-start(bf16[128,3584]{1,0:T(8,128)(2,1)} %refs_8_.9), channel_id=1, source_target_pairs={{0,8},{8,0},{16,24},{24,16},{1,9},{9,1},{17,25},{25,17},{2,10},{10... | collective-permute-start | bytes 2752520 | tf_op jit(solution)/shard_map/ppermute | solution.py:57
  13.2 17.3 %copy-start.2 = (bf16[64,2048]{1,0:T(8,128)(2,1)}, bf16[64,2048]{1,0:T(8,128)(2,1)S(1)}, u32[]{:S(2)}) copy-start(bf16[64,2048]{1,0:T(8,128)(2,1)S(1)} %collective-permute-done.5.refs_6_) | copy-start | bytes 786436
  13.2 45.1 %collective-permute-start.16 = (bf16[128,3584]{1,0:T(8,128)(2,1)}, bf16[128,3584]{1,0:T(8,128)(2,1)S(1)}, u32[]{:S(2)}, u32[]{:S(2)}) collective-permute-start(bf16[128,3584]{1,0:T(8,128)(2,1)} %refs_8_.9), channel_id=1, source_target_pairs={{0,16},{8,24},{16,0},{24,8},{1,17},{9,25},{17,1},{25,9},{2,18},{10... | collective-permute-start | bytes 2752520 | tf_op jit(solution)/shard_map/ppermute | solution.py:57
  28.3 2.3 %copy-start.3 = (bf16[64,2048]{1,0:T(8,128)(2,1)}, bf16[64,2048]{1,0:T(8,128)(2,1)S(1)}, u32[]{:S(2)}) copy-start(bf16[64,2048]{1,0:T(8,128)(2,1)S(1)} %collective-permute-done.3.refs_4_) | copy-start | bytes 786436
  28.3 1.5 %collective-permute-start.6 = (bf16[64,2048]{1,0:T(8,128)(2,1)S(1)}, bf16[64,2048]{1,0:T(8,128)(2,1)S(1)}, u32[]{:S(2)}, u32[]{:S(2)}) collective-permute-start(bf16[64,2048]{1,0:T(8,128)(2,1)S(1)} %collective-permute-done.5.refs_6_), channel_id=1, source_target_pairs={{0,1},{1,0},{2,3},{3,2},{4,5},{5,4},{6,7},{7,6},{8,9},{9,8},{10,11... | collective-permute-start | bytes 786440 | tf_op jit(solution)/shard_map/ppermute | solution.py:71
  28.3 2.3 %copy-start.4 = (bf16[64,2048]{1,0:T(8,128)(2,1)}, bf16[64,2048]{1,0:T(8,128)(2,1)S(1)}, u32[]{:S(2)}) copy-start(bf16[64,2048]{1,0:T(8,128)(2,1)S(1)} %collective-permute-done.1.refs_2_) | copy-start | bytes 786436
  28.3 1.9 %collective-permute-start.4 = (bf16[64,2048]{1,0:T(8,128)(2,1)S(1)}, bf16[64,2048]{1,0:T(8,128)(2,1)S(1)}, u32[]{:S(2)}, u32[]{:S(2)}) collective-permute-start(bf16[64,2048]{1,0:T(8,128)(2,1)S(1)} %collective-permute-done.3.refs_4_), channel_id=1, source_target_pairs={{0,1},{1,0},{2,3},{3,2},{4,5},{5,4},{6,7},{7,6},{8,9},{9,8},{10,11... | collective-permute-start | bytes 786440 | tf_op jit(solution)/shard_map/ppermute | solution.py:71
  28.8 1.8 %copy-start.5 = (bf16[64,2048]{1,0:T(8,128)(2,1)}, bf16[64,2048]{1,0:T(8,128)(2,1)S(1)}, u32[]{:S(2)}) copy-start(bf16[64,2048]{1,0:T(8,128)(2,1)S(1)} %collective-permute-done.refs_1_) | copy-start | bytes 786436
  28.8 1.8 %collective-permute-start.2 = (bf16[64,2048]{1,0:T(8,128)(2,1)S(1)}, bf16[64,2048]{1,0:T(8,128)(2,1)S(1)}, u32[]{:S(2)}, u32[]{:S(2)}) collective-permute-start(bf16[64,2048]{1,0:T(8,128)(2,1)S(1)} %collective-permute-done.1.refs_2_), channel_id=1, source_target_pairs={{0,1},{1,0},{2,3},{3,2},{4,5},{5,4},{6,7},{7,6},{8,9},{9,8},{10,11... | collective-permute-start | bytes 786440 | tf_op jit(solution)/shard_map/ppermute | solution.py:71
  29.8 0.8 copy-start.6
  30.2 0.7 copy-start.7
  30.9 0.7 copy-start.8
  38.1 27.4 %collective-permute-start.13 = (bf16[272,768]{1,0:T(8,128)(2,1)}, bf16[272,768]{1,0:T(8,128)(2,1)S(1)}, u32[]{:S(2)}, u32[]{:S(2)}) collective-permute-start(bf16[272,768]{1,0:T(8,128)(2,1)} %get-tuple-element.17), channel_id=1, source_target_pairs={{0,16},{8,24},{16,0},{24,8},{1,17},{9,25},{17,1},{25,9},{2,18},{10... | collective-permute-start | bytes 1253384 | tf_op jit(solution)/shard_map/ppermute | solution.py:57
  47.2 45.0 %collective-permute-start.9 = (bf16[272,1024]{1,0:T(8,128)(2,1)}, bf16[272,1024]{1,0:T(8,128)(2,1)S(1)}, u32[]{:S(2)}, u32[]{:S(2)}) collective-permute-start(bf16[272,1024]{1,0:T(8,128)(2,1)} %get-tuple-element.13), channel_id=1, source_target_pairs={{0,16},{8,24},{16,0},{24,8},{1,17},{9,25},{17,1},{25,9},{2,18},{10... | collective-permute-start | bytes 1671176 | tf_op jit(solution)/shard_map/ppermute | solution.py:57
  55.2 41.0 %collective-permute-start.7 = (bf16[272,1024]{1,0:T(8,128)(2,1)}, bf16[272,1024]{1,0:T(8,128)(2,1)S(1)}, u32[]{:S(2)}, u32[]{:S(2)}) collective-permute-start(bf16[272,1024]{1,0:T(8,128)(2,1)} %get-tuple-element.11), channel_id=1, source_target_pairs={{0,8},{8,0},{16,24},{24,16},{1,9},{9,1},{17,25},{25,17},{2,10},{10... | collective-permute-start | bytes 1671176 | tf_op jit(solution)/shard_map/ppermute | solution.py:57
  56.7 43.7 %copy-start.13 = (bf16[128,3584]{1,0:T(8,128)(2,1)}, bf16[128,3584]{1,0:T(8,128)(2,1)S(1)}, u32[]{:S(2)}) copy-start(bf16[128,3584]{1,0:T(8,128)(2,1)S(1)} %collective-permute-done.15.refs_9_) | copy-start | bytes 2752516
  56.8 42.8 %collective-permute-start.17 = (bf16[64,3584]{1,0:T(8,128)(2,1)S(1)}, bf16[64,3584]{1,0:T(8,128)(2,1)S(1)}, u32[]{:S(2)}, u32[]{:S(2)}) collective-permute-start(bf16[64,3584]{1,0:T(8,128)(2,1)S(1)} %slice.8), channel_id=1, source_target_pairs={{0,16},{8,24},{16,0},{24,8},{1,17},{9,25},{17,1},{25,9},{2,18},{10... | collective-permute-start | bytes 1376264 | tf_op jit(solution)/shard_map/ppermute | solution.py:57
  58.4 42.0 %copy-start.14 = (bf16[128,3584]{1,0:T(8,128)(2,1)}, bf16[128,3584]{1,0:T(8,128)(2,1)S(1)}, u32[]{:S(2)}) copy-start(bf16[128,3584]{1,0:T(8,128)(2,1)S(1)} %collective-permute-done.16.refs_10_) | copy-start | bytes 2752516
  58.4 42.0 %collective-permute-start.18 = (bf16[64,3584]{1,0:T(8,128)(2,1)S(1)}, bf16[64,3584]{1,0:T(8,128)(2,1)S(1)}, u32[]{:S(2)}, u32[]{:S(2)}) collective-permute-start(bf16[64,3584]{1,0:T(8,128)(2,1)S(1)} %slice.9), channel_id=1, source_target_pairs={{0,8},{8,0},{16,24},{24,16},{1,9},{9,1},{17,25},{25,17},{2,10},{10... | collective-permute-start | bytes 1376264 | tf_op jit(solution)/shard_map/ppermute | solution.py:57
  65.5 1.6 %copy-start.9 = (bf16[272,768]{1,0:T(8,128)(2,1)}, bf16[272,768]{1,0:T(8,128)(2,1)S(1)}, u32[]{:S(2)}) copy-start(bf16[272,768]{1,0:T(8,128)(2,1)S(1)} %collective-permute-done.13.refs_0_.refs_13_.refs_14_) | copy-start | bytes 1253380
  65.6 22.8 %collective-permute-start.11 = (bf16[272,768]{1,0:T(8,128)(2,1)}, bf16[272,768]{1,0:T(8,128)(2,1)S(1)}, u32[]{:S(2)}, u32[]{:S(2)}) collective-permute-start(bf16[272,768]{1,0:T(8,128)(2,1)} %get-tuple-element.15), channel_id=1, source_target_pairs={{0,8},{8,0},{16,24},{24,16},{1,9},{9,1},{17,25},{25,17},{2,10},{10... | collective-permute-start | bytes 1253384 | tf_op jit(solution)/shard_map/ppermute | solution.py:57
  88.4 1.5 %copy-start.10 = (bf16[272,768]{1,0:T(8,128)(2,1)}, bf16[272,768]{1,0:T(8,128)(2,1)S(1)}, u32[]{:S(2)}) copy-start(bf16[272,768]{1,0:T(8,128)(2,1)S(1)} %collective-permute-done.11.refs_0_.refs_9_.refs_10_) | copy-start | bytes 1253380
  88.4 29.8 %collective-permute-start.14 = (bf16[144,768]{1,0:T(8,128)(2,1)}, bf16[144,768]{1,0:T(8,128)(2,1)S(1)}, u32[]{:S(2)}, u32[]{:S(2)}) collective-permute-start(bf16[144,768]{1,0:T(8,128)(2,1)} %combine.7), channel_id=1, source_target_pairs={{0,8},{8,0},{16,24},{24,16},{1,9},{9,1},{17,25},{25,17},{2,10},{10... | collective-permute-start | bytes 663560 | tf_op jit(solution)/shard_map/ppermute | solution.py:57
  92.1 1.5 %copy-start = (bf16[272,1024]{1,0:T(8,128)(2,1)}, bf16[272,1024]{1,0:T(8,128)(2,1)S(1)}, u32[]{:S(2)}) copy-start(bf16[272,1024]{1,0:T(8,128)(2,1)S(1)} %collective-permute-done.9.refs_0_.refs_5_.refs_6_) | copy-start | bytes 1671172
  92.1 26.1 %collective-permute-start.12 = (bf16[144,768]{1,0:T(8,128)(2,1)}, bf16[144,768]{1,0:T(8,128)(2,1)S(1)}, u32[]{:S(2)}, u32[]{:S(2)}) collective-permute-start(bf16[144,768]{1,0:T(8,128)(2,1)} %combine.6), channel_id=1, source_target_pairs={{0,16},{8,24},{16,0},{24,8},{1,17},{9,25},{17,1},{25,9},{2,18},{10... | collective-permute-start | bytes 663560 | tf_op jit(solution)/shard_map/ppermute | solution.py:57
  96.2 0.8 copy-start.1
  96.2 22.0 %collective-permute-start.10 = (bf16[144,1024]{1,0:T(8,128)(2,1)}, bf16[144,1024]{1,0:T(8,128)(2,1)S(1)}, u32[]{:S(2)}, u32[]{:S(2)}) collective-permute-start(bf16[144,1024]{1,0:T(8,128)(2,1)} %combine.5), channel_id=1, source_target_pairs={{0,8},{8,0},{16,24},{24,16},{1,9},{9,1},{17,25},{25,17},{2,10},{10... | collective-permute-start | bytes 884744 | tf_op jit(solution)/shard_map/ppermute | solution.py:57
  99.6 0.8 copy-start.17
  99.6 18.7 %collective-permute-start.8 = (bf16[144,1024]{1,0:T(8,128)(2,1)}, bf16[144,1024]{1,0:T(8,128)(2,1)S(1)}, u32[]{:S(2)}, u32[]{:S(2)}) collective-permute-start(bf16[144,1024]{1,0:T(8,128)(2,1)} %combine.4), channel_id=1, source_target_pairs={{0,16},{8,24},{16,0},{24,8},{1,17},{9,25},{17,1},{25,9},{2,18},{10... | collective-permute-start | bytes 884744 | tf_op jit(solution)/shard_map/ppermute | solution.py:57
  100.4 0.8 copy-start.18
  118.2 0.7 copy-start.15
  118.2 0.8 copy-start.16
  118.3 0.9 copy-start.11
  119.1 0.7 copy-start.12

commit v2 on v0

v2 whole, which is shorter than its diff:
```python
import functools

import jax
import jax.numpy as jnp
from jax import lax
from jax.experimental import pallas as pl
from jax.experimental.pallas import tpu as pltpu
from jax.sharding import PartitionSpec as P

CORES = 2
SPAN = 120.0
SCALE_ROWS = 16
COST = 1024
SCOPED = 20 * 1024 * 1024
ANY, HBM, VMEM = pl.ANY, pltpu.HBM, pltpu.VMEM
MARK = ((8, 128), jnp.float32, VMEM)


def call(kernel, name, operands, results, scratch=(), aliases={}):
    return pl.pallas_call(
        kernel,
        in_specs=[pl.BlockSpec(memory_space=memory) for _, memory in operands],
        out_specs=[pl.BlockSpec(memory_space=memory) for _, _, memory in results],
        out_shape=[
            jax.ShapeDtypeStruct(shape, dtype) if memory is ANY else memory(shape, dtype)
            for shape, dtype, memory in results
        ],
        scratch_shapes=list(scratch),
        input_output_aliases=aliases,
        compiler_params=pltpu.CompilerParams(vmem_limit_bytes=SCOPED),
        cost_estimate=pl.CostEstimate(flops=COST, bytes_accessed=COST, transcendentals=0),
        name=name,
    )(*[pltpu.with_memory_space_constraint(array, memory) for array, memory in operands])


def grid_of(n):
    ny = int(n**0.5)
    while n % ny:
        ny -= 1
    return ny, n // ny


def encode(blocks):
    top = functools.reduce(jnp.maximum, [jnp.max(jnp.abs(block), axis=0, keepdims=True) for block in blocks])
    scale = jnp.maximum(top * 1.0078125, 1e-36).astype(jnp.bfloat16)
    step = 2 * SPAN / scale.astype(jnp.float32)
    codes = []
    for block in blocks:
        size = jnp.exp2(jnp.abs(block) * step - SPAN)
        codes.append(jnp.where(block < 0, -size, size).astype(jnp.bfloat16))
    return codes, scale


def decode(code, scale):
    value = code.astype(jnp.float32)
    size = (jnp.log2(jnp.abs(value)) + SPAN) * (scale.astype(jnp.float32)[:1] * (0.5 / SPAN))
    return jnp.where(value < 0, -size, size)


def store_message(ref, blocks, columns):
    codes, scale = encode(blocks)
    at = 0
    for code in codes:
        ref[at : at + code.shape[0], columns] = code
        at += code.shape[0]
    ref[at:, columns] = jnp.broadcast_to(scale, (SCALE_ROWS, scale.shape[1]))


class Plan:
    def __init__(self, mesh):
        self.n, self.m = mesh.shape["row"], mesh.shape["col"]
        self.ny, self.nx = grid_of(self.n)
        self.nz = self.m // CORES

    def place(self):
        row, col = lax.axis_index("row"), lax.axis_index("col")
        return row // self.nx, row % self.nx, col // CORES, col % CORES

    def send_row(self, array, dy, dx):
        ny, nx = self.ny, self.nx
        pairs = [(y * nx + x, (y + dy) % ny * nx + (x + dx) % nx) for y in range(ny) for x in range(nx)]
        return lax.ppermute(array, "row", pairs)

    def peer_z(self, z, d):
        return z ^ d if self.nz & (self.nz - 1) == 0 else (z + d) % self.nz

    def from_z(self, z, d):
        return z ^ d if self.nz & (self.nz - 1) == 0 else (z + self.nz - d) % self.nz

    def send_z(self, array, d):
        pairs = [(z * CORES + c, self.peer_z(z, d) * CORES + c) for z in range(self.nz) for c in range(CORES)]
        return lax.ppermute(array, "col", pairs)

    def swap(self, array, d):
        pairs = [(z * CORES + c, z * CORES + (c + d) % CORES) for z in range(self.nz) for c in range(CORES)]
        return lax.ppermute(array, "col", pairs)

    def token_copies(self, pieces, held, sems):
        y, x, z, core = self.place()
        rows = pieces[0].shape[0]
        per = self.m // self.n
        copies = []
        for at in range(len(pieces)):
            d, c = at // CORES, at % CORES
            origin = self.from_z(z, d) * CORES + lax.rem(core + CORES - c, CORES)
            owner = origin // per
            dy = lax.rem(owner // self.nx + self.ny - y, self.ny)
            dx = lax.rem(owner % self.nx + self.nx - x, self.nx)
            start = pl.multiple_of(((dy * self.nx + dx) * per + origin % per) * rows, rows)
            copies.append(pltpu.make_async_copy(pieces[at], held.at[pl.ds(start, rows), :], sems.at[at]))
        return copies

    def stage(self, weight, relay):
        def kernel(weight_ref, *refs):
            out, _, sem = refs[-3:]
            copy = pltpu.make_async_copy(weight_ref, out, sem)
            copy.start()
            copy.wait()

        return call(
            kernel,
            "stage",
            [(weight, HBM), (relay, ANY)],
            [(weight.shape, weight.dtype, VMEM), (relay.shape, relay.dtype, ANY)],
            [pltpu.SemaphoreType.DMA],
            aliases={1: 1},
        )

    def relay(self, array, after):
        operands = [(array, ANY)] + [(other, VMEM) for other in after]
        return call(lambda *refs: None, "relay", operands, [(array.shape, array.dtype, ANY)], aliases={0: 0})[0]

    def gather_tokens(self, pieces, after):
        count, (rows, depth) = len(pieces), pieces[0].shape

        def kernel(*refs):
            out, sems = refs[-2:]
            copies = self.token_copies(refs[:count], out, sems)
            for copy in copies:
                copy.start()
            for copy in copies:
                copy.wait()

        return call(
            kernel,
            "gather_tokens",
            [(piece, ANY) for piece in pieces] + [(array, ANY) for array in after],
            [((count * rows, depth), jnp.bfloat16, VMEM)],
            [pltpu.SemaphoreType.DMA((count,))],
        )[0]

    def gather_hidden(self, blocks, after):
        count, units = len(blocks), blocks[0].shape[1]
        tokens = sum(block.shape[0] for block in blocks)

        def kernel(*refs):
            out, sems = refs[-2:]
            copies, at = [], 0
            for index, ref in enumerate(refs[:count]):
                rows = ref.shape[0]
                copies.append(pltpu.make_async_copy(ref, out.at[pl.ds(at, rows), :], sems.at[index]))
                at += rows
            for copy in copies:
                copy.start()
            for copy in copies:
                copy.wait()

        return call(
            kernel,
            "gather_hidden",
            [(block, ANY) for block in blocks] + [(array, VMEM) for array in after],
            [((tokens, units), jnp.bfloat16, VMEM)],
            [pltpu.SemaphoreType.DMA((count,))],
        )[0]

    def token_part(self, held, weight, first, width, tile, x_first, after):
        tokens, depth = held.shape
        own = tokens // self.n
        peers, blocks = (self.nx, self.ny) if x_first else (self.ny, self.nx)
        group = blocks * own

        def kernel(held_ref, weight_ref, *refs):
            outs = refs[len(after) :]
            messages, keep = outs[:-1], outs[-1]
            for at in range(0, width, tile):
                size = min(tile, width - at)
                columns = slice(at, at + size)
                total = lax.dot_general(
                    held_ref[...],
                    weight_ref[first + at : first + at + size, :],
                    (((1,), (1,)), ((), ())),
                    preferred_element_type=jnp.float32,
                )

                def block(peer, at):
                    slot = at * self.nx + peer if x_first else peer * self.nx + at
                    return total[slot * own : (slot + 1) * own]

                for peer in range(1, peers):
                    store_message(messages[peer - 1], [block(peer, at) for at in range(blocks)], columns)
                for at in range(blocks):
                    keep[at * own : (at + 1) * own, columns] = block(0, at)

        *messages, keep = call(
            kernel,
            "token_part",
            [(held, VMEM), (weight, VMEM)] + [(array, VMEM) for array in after],
            [((group + SCALE_ROWS, width), jnp.bfloat16, VMEM)] * (peers - 1) + [((group, width), jnp.float32, VMEM)],
        )
        return messages, keep

    def combine(self, got, keep, blocks, after):
        count, (group, width) = len(got), keep.shape
        own = group // blocks

        def kernel(*refs):
            messages, keep_ref, outs = refs[:count], refs[count], refs[count + 1 + len(after) :]
            for block in range(1, blocks):
                rows = slice(block * own, (block + 1) * own)
                total = keep_ref[rows, :]
                for message in messages:
                    total = total + decode(message[rows, :], message[group:, :])
                store_message(outs[block - 1], [total], slice(None))

        return call(
            kernel,
            "combine",
            [(array, VMEM) for array in (*got, keep, *after)],
            [((own + SCALE_ROWS, width), jnp.bfloat16, VMEM)] * (blocks - 1),
        )

    def finish(self, first, keep, got, late, own, units, so_far, after):
        group, width = keep.shape
        operands = [(array, VMEM) for array in (keep, *got, *late, *after)]
        extra = [(so_far, HBM)] if so_far is not None else []

        def kernel(*refs):
            total = refs[0][:own, :]
            for message in refs[1 : 1 + len(got)]:
                total = total + decode(message[:own, :], message[group:, :])
            for message in refs[1 + len(got) : 1 + len(got) + len(late)]:
                total = total + decode(message[:own, :], message[own:, :])
            out, _, buf, sem = refs[-4:]
            buf[...] = total.astype(jnp.bfloat16)
            copy = pltpu.make_async_copy(buf, out.at[:, pl.ds(first, width)], sem)
            copy.start()
            copy.wait()

        return call(
            kernel,
            "finish",
            operands + extra,
            [((own, units), jnp.bfloat16, HBM), MARK],
            [pltpu.VMEM((own, width), jnp.bfloat16), pltpu.SemaphoreType.DMA],
            aliases={len(operands): 0} if extra else {},
        )

    def weight_part(self, held, hidden, first, width, tile, so_far, after):
        (tokens, depth), units = held.shape, hidden.shape[1]
        steps = width // tile
        extra = [(so_far, HBM)] if so_far is not None else []
        operands = [(array, VMEM) for array in (held, hidden, *after)]

        def kernel(held_ref, hidden_ref, *refs):
            out, _, buf, sems = refs[-4:]
            pending = []
            for s in range(steps):
                if s >= 2:
                    pending[s - 2].wait()
                start = first + s * tile
                buf[s % 2] = lax.dot_general(
                    hidden_ref[:, start : start + tile],
                    held_ref[...],
                    (((0,), (0,)), ((), ())),
                    preferred_element_type=jnp.float32,
                ).astype(jnp.bfloat16)
                pending.append(pltpu.make_async_copy(buf.at[s % 2], out.at[pl.ds(start, tile), :], sems.at[s % 2]))
                pending[-1].start()
            for copy in pending[-2:]:
                copy.wait()

        return call(
            kernel,
            "weight_part",
            operands + extra,
            [((units, depth), jnp.bfloat16, HBM), MARK],
            [pltpu.VMEM((2, tile, depth), jnp.bfloat16), pltpu.SemaphoreType.DMA((2,))],
            aliases={len(operands): 0} if extra else {},
        )


def split(total, tile, parts):
    tiles = total // tile
    parts = min(parts, tiles)
    sizes = [tiles // parts + (at < tiles % parts) for at in range(parts)]
    return [(sum(sizes[:at]) * tile, size * tile) for at, size in enumerate(sizes)]


def on_device(plan, out_grad, hidden, weight):
    ny, nx = plan.ny, plan.nx
    pieces = []
    for d in range(plan.nz):
        piece = plan.send_z(out_grad, d) if d else out_grad
        if d == 1:
            weight, piece = plan.stage(weight, piece)
        elif d:
            piece = plan.relay(piece, [weight])
        pieces += [piece] + [plan.swap(piece, c) for c in range(1, CORES)]

    own, units = hidden.shape
    half = own // 2
    at_x = [hidden] + [plan.send_row(hidden, 0, dx) for dx in range(1, nx)]
    at_y = [hidden] + [plan.send_row(hidden, dy, 0) for dy in range(1, ny)]

    def block_of(dy, dx):
        if dy == 0:
            return [at_x[dx]]
        if dx == 0:
            return [at_y[dy]]
        return [plan.send_row(at_x[dx][:half], dy, 0), plan.send_row(at_y[dy][half:], 0, dx)]

    blocks = []
    for sy in range(ny):
        for sx in range(nx):
            blocks += block_of((ny - sy) % ny, (nx - sx) % nx)

    tile = 256 if units % 256 == 0 else 128
    chunks, rows = split(units, tile, 4), split(units, tile, 2)
    weight_grad = token_grad = None
    held = plan.gather_tokens(pieces, [])
    last, parts, lates, gathered = [], [], [], None

    def part(at):
        nonlocal last
        (first, width), x_first = chunks[at], at % 2 == 0
        messages, keep = plan.token_part(held, weight, first, width, 2 * tile, x_first, last)
        last = [keep]
        got = [plan.send_row(msg, 0, d + 1) if x_first else plan.send_row(msg, d + 1, 0) for d, msg in enumerate(messages)]
        parts.append((keep, got))

    def collect(at):
        nonlocal last, gathered
        gathered = plan.gather_hidden(blocks, last)
        last = [gathered]

    def join(at):
        nonlocal last
        x_first = at % 2 == 0
        keep, got = parts[at]
        onward = plan.combine(got, keep, ny if x_first else nx, last)
        last = list(onward[:1])
        lates.append([plan.send_row(msg, d + 1, 0) if x_first else plan.send_row(msg, 0, d + 1) for d, msg in enumerate(onward)])

    def weigh(at):
        nonlocal last, weight_grad
        first, width = rows[at]
        weight_grad, mark = plan.weight_part(held, gathered, first, width, tile, weight_grad, last)
        last = [mark]

    def end(at):
        nonlocal last, token_grad
        token_grad, mark = plan.finish(chunks[at][0], *parts[at], lates[at], own, units, token_grad, last)
        last = [mark]

    for name, at in PROGRAM:
        if at < len(chunks):
            {"part": part, "collect": collect, "join": join, "weigh": weigh, "end": end}[name](at)
    return token_grad, weight_grad


PROGRAM = [
    ("part", 0),
    ("part", 1),
    ("collect", 0),
    ("part", 2),
    ("part", 3),
    ("weigh", 0),
    ("join", 0),
    ("join", 1),
    ("join", 2),
    ("join", 3),
    ("weigh", 1),
    ("end", 0),
    ("end", 1),
    ("end", 2),
    ("end", 3),
]


def solution(mesh):
    return jax.shard_map(
        functools.partial(on_device, Plan(mesh)),
        mesh=mesh,
        in_specs=(P("col", "row"), P("row", "col"), P("col", "row")),
        out_specs=(P("row", "col"), P("col", "row")),
        check_vma=False,
    )
```

time: 650 us -> 79.6 us (0.12)
  waiting for transfers between devices: 550 us -> 21.3 us
  matrix products: 42.4 us -> 0 us
  blocking collectives: 40.4 us -> 0 us
  Pallas kernels: 0 us -> 36 us
  starting transfers between devices: 0.11 us -> 20 us
  between operations: 13.7 us -> 1 us
    all_gather x3 -> x0, waiting for transfers between devices: 548 us -> none  [the longest x1 493 us: on_device(): lax.all_gather(weight, 'row', axis=1, tiled=True)]
    dot_general x2 -> x0, matrix products: 42.4 us -> none  [the longest x1 26.5 us: on_device(): lax.dot_general(cotangent, lax.all_gather(weight, 'row', axis=1, tiled=Tr...]
    all_to_all x1 -> x0, blocking collectives: 40.4 us -> none  [on_device(): lax.all_to_all(gathered, 'row', split_axis=0, concat_axis=1, tiled=True)]
    pallas_call x0 -> x19, Pallas kernels: none -> 36 us  [call(): pl.pallas_call(kernel, in_specs=[pl.BlockSpec(memory_space=memory) for _,...]
    ppermute x0 -> x19, waiting for transfers between devices: none -> 21.3 us  [the longest x3 13.6 us: send_z(): return lax.ppermute(array, 'col', pairs)]
    ppermute x0 -> x19, starting transfers between devices: none -> 20 us  [the longest x12 15.1 us: send_row(): return lax.ppermute(array, 'row', pairs)]
  transfers between devices with their start and end apart: 3 -> 19, of which waited for: 3 -> 6; matrix products, arithmetic and copies ran while one was open for 3% -> 0% of each run, Pallas kernels for 0% -> 44%
where the time goes in v2:
time: 79.6 us; the launch traced here: 78.3 us
  Pallas kernels  36 us (45%)
  waiting for transfers between devices  21.3 us (27%)
  starting transfers between devices  20 us (25%)
  between operations  1 us (1%)
    pallas_call x19, Pallas kernels, call(): pl.pallas_call(kernel, in_specs=[pl.BlockSpec(memory_space=memory) for _,...  36 us
    ppermute x12, starting transfers between devices, send_row(): return lax.ppermute(array, 'row', pairs)  15.1 us
    ppermute x3, waiting for transfers between devices, send_z(): return lax.ppermute(array, 'col', pairs)  13.6 us
    ppermute x12, waiting for transfers between devices, send_row(): return lax.ppermute(array, 'row', pairs)  7.24 us
    ppermute x3, starting transfers between devices, send_z(): return lax.ppermute(array, 'col', pairs)  4.39 us
  transfers between devices with their start and end apart: 19, of which 6 were waited for; matrix products, arithmetic and copies ran while one was open for 0% of the time, Pallas kernels for 44%

profile of v2, /device:TPU:0, one launch (start us, length us, event | category | flops | bytes accessed | tf_op | source)
XLA Modules:
  0.0 78.3 jit_solution(12423553209051096779)
XLA Ops:
  0.6 3.0 %collective-permute-start.7 = (bf16[128,3584]{1,0:T(8,128)(2,1)}, bf16[128,3584]{1,0:T(8,128)(2,1)S(1)}, u32[]{:S(2)}, u32[]{:S(2)}) collective-permute-start(bf16[128,3584]{1,0:T(8,128)(2,1)} %refs_0_.3), channel_id=1, source_target_pairs={{0,8},{8,0},{16,24},{24,16},{1,9},{9,1},{17,25},{25,17},{2,10},{10... | collective-permute-start | bytes 2752520 | tf_op jit(solution)/shard_map/ppermute | solution.py:82
  3.6 1.5 %collective-permute-start.8 = (bf16[128,3584]{1,0:T(8,128)(2,1)}, bf16[128,3584]{1,0:T(8,128)(2,1)S(1)}, u32[]{:S(2)}, u32[]{:S(2)}) collective-permute-start(bf16[128,3584]{1,0:T(8,128)(2,1)} %refs_0_.3), channel_id=1, source_target_pairs={{0,16},{8,24},{16,0},{24,8},{1,17},{9,25},{17,1},{25,9},{2,18},{10... | collective-permute-start | bytes 2752520 | tf_op jit(solution)/shard_map/ppermute | solution.py:82
  5.2 1.6 %collective-permute-start.1 = (bf16[64,2048]{1,0:T(8,128)(2,1)}, bf16[64,2048]{1,0:T(8,128)(2,1)S(1)}, u32[]{:S(2)}, u32[]{:S(2)}) collective-permute-start(bf16[64,2048]{1,0:T(8,128)(2,1)} %refs_0_.2), channel_id=1, source_target_pairs={{0,2},{1,3},{2,0},{3,1},{4,6},{5,7},{6,4},{7,5},{8,10},{9,11},{10,... | collective-permute-start | bytes 786440 | tf_op jit(solution)/shard_map/ppermute | solution.py:92
  6.7 2.6 %collective-permute-start.3 = (bf16[64,2048]{1,0:T(8,128)(2,1)}, bf16[64,2048]{1,0:T(8,128)(2,1)S(1)}, u32[]{:S(2)}, u32[]{:S(2)}) collective-permute-start(bf16[64,2048]{1,0:T(8,128)(2,1)} %refs_0_.2), channel_id=1, source_target_pairs={{0,4},{1,5},{2,6},{3,7},{4,0},{5,1},{6,2},{7,3},{8,12},{9,13},{10,... | collective-permute-start | bytes 786440 | tf_op jit(solution)/shard_map/ppermute | solution.py:92
  9.3 0.2 collective-permute-start.5
  9.5 7.9 %collective-permute-done.1.refs_0_ = bf16[64,2048]{1,0:T(8,128)(2,1)S(1)} collective-permute-done((bf16[64,2048]{1,0:T(8,128)(2,1)}, bf16[64,2048]{1,0:T(8,128)(2,1)S(1)}, u32[]{:S(2)}, u32[]{:S(2)}) %collective-permute-start.1) | collective-permute-done | bytes 262176 | tf_op jit(solution)/shard_map/ppermute | solution.py:92
  17.4 0.0 collective-permute-start
  17.4 5.2 %stage.1 = (bf16[3584,2048]{1,0:T(8,128)(2,1)S(1)}, bf16[64,2048]{1,0:T(8,128)(2,1)S(1)}) custom-call(bf16[3584,2048]{1,0:T(8,128)(2,1)} %weight_ref.1, bf16[64,2048]{1,0:T(8,128)(2,1)S(1)} %collective-permute-done.1.refs_0_), custom_call_target="tpu_custom_call", output_to_operand_aliasing={{1}: (1, {})} | custom-call | flops 1024 | bytes 1024 | tf_op jit(solution)/shard_map/stage/pallas_call | solution.py:20
  22.6 5.7 %collective-permute-done.3.refs_0_ = bf16[64,2048]{1,0:T(8,128)(2,1)S(1)} collective-permute-done((bf16[64,2048]{1,0:T(8,128)(2,1)}, bf16[64,2048]{1,0:T(8,128)(2,1)S(1)}, u32[]{:S(2)}, u32[]{:S(2)}) %collective-permute-start.3) | collective-permute-done | bytes 262176 | tf_op jit(solution)/shard_map/ppermute | solution.py:92
  28.3 0.0 copy-start.1
  28.3 0.0 collective-permute-start.4
  28.3 0.0 collective-permute-done.5.refs_0_
  28.3 0.5 collective-permute-start.6
  28.8 0.0 collective-permute-done.7.refs_1_
  28.8 0.1 collective-permute-start.2
  29.0 0.0 collective-permute-done.8.refs_2_
  29.0 0.6 collective-permute-start.9
  29.6 0.0 collective-permute-done.refs_1_
  29.6 0.6 collective-permute-start.10
  30.2 0.0 collective-permute-done.4.refs_5_
  30.2 0.0 collective-permute-done.6.refs_7_
  30.2 0.4 collective-permute-done.2.refs_3_
  30.6 0.0 copy-done.1
  30.6 0.2 gather_tokens.1.held_ref
  30.9 0.0 copy-start
  30.9 2.7 %token_part.4 = (bf16[272,1024]{1,0:T(8,128)(2,1)S(1)}, f32[256,1024]{1,0:T(8,128)S(1)}) custom-call(bf16[512,2048]{1,0:T(8,128)(2,1)S(1)} %gather_tokens.1.held_ref, bf16[3584,2048]{1,0:T(8,128)(2,1)S(1)} %get-tuple-element.24.refs_1_.weight_ref), custom_call_target="tpu_custom_call" | custom-call | flops 1024 | bytes 1024 | tf_op jit(solution)/shard_map/token_part/pallas_call | solution.py:20
  33.6 1.3 %collective-permute-start.14 = (bf16[272,1024]{1,0:T(8,128)(2,1)S(1)}, bf16[272,1024]{1,0:T(8,128)(2,1)S(1)}, u32[]{:S(2)}, u32[]{:S(2)}) collective-permute-start(bf16[272,1024]{1,0:T(8,128)(2,1)S(1)} %get-tuple-element.32), channel_id=1, source_target_pairs={{0,8},{8,0},{16,24},{24,16},{1,9},{9,1},{17,25},{25,17},{2,10},{10... | collective-permute-start | bytes 1671176 | tf_op jit(solution)/shard_map/ppermute | solution.py:82
  34.9 2.7 %token_part.5 = (bf16[272,1024]{1,0:T(8,128)(2,1)S(1)}, f32[256,1024]{1,0:T(8,128)S(1)}) custom-call(bf16[512,2048]{1,0:T(8,128)(2,1)S(1)} %gather_tokens.1.held_ref, bf16[3584,2048]{1,0:T(8,128)(2,1)S(1)} %get-tuple-element.24.refs_1_.weight_ref, f32[256,1024]{1,0:T(8,128)S(1)} %get-tuple-element.25.refs_0_.refs_1_), custom_call_target="tpu_custom_call" | custom-call | flops 1024 | bytes 1024 | tf_op jit(solution)/shard_map/token_part/pallas_call | solution.py:20
  37.6 1.6 %collective-permute-start.13 = (bf16[272,1024]{1,0:T(8,128)(2,1)S(1)}, bf16[272,1024]{1,0:T(8,128)(2,1)S(1)}, u32[]{:S(2)}, u32[]{:S(2)}) collective-permute-start(bf16[272,1024]{1,0:T(8,128)(2,1)S(1)} %get-tuple-element.31), channel_id=1, source_target_pairs={{0,16},{8,24},{16,0},{24,8},{1,17},{9,25},{17,1},{25,9},{2,18},{10... | collective-permute-start | bytes 1671176 | tf_op jit(solution)/shard_map/ppermute | solution.py:82
  39.2 3.2 %collective-permute-done.9.refs_3_ = bf16[64,3584]{1,0:T(8,128)(2,1)S(1)} collective-permute-done((bf16[64,3584]{1,0:T(8,128)(2,1)S(1)}, bf16[64,3584]{1,0:T(8,128)(2,1)S(1)}, u32[]{:S(2)}, u32[]{:S(2)}) %collective-permute-start.9) | collective-permute-done | bytes 458784 | tf_op jit(solution)/shard_map/ppermute | solution.py:82
  42.4 0.7 collective-permute-done.10.refs_4_
  43.0 0.0 copy-done
  43.0 1.4 %gather_hidden.1.refs_0_.hidden_ref = bf16[512,3584]{1,0:T(8,128)(2,1)S(1)} custom-call(bf16[128,3584]{1,0:T(8,128)(2,1)S(1)} %copy-done, bf16[128,3584]{1,0:T(8,128)(2,1)S(1)} %collective-permute-done.7.refs_1_, bf16[128,3584]{1,0:T(8,128)(2,1)S(1)} %collective-permute-done.8.refs_2_, bf16[64,3584]{1,0:T(8,128)(2,1)S(1)} %collective-permute-done.9.refs_3_, ...), custom_call_target="tpu_custom_call" | custom-call | flops 1024 | bytes 1024 | tf_op jit(solution)/shard_map/gather_hidden/pallas_call | solution.py:20
  44.5 2.0 %token_part.6 = (bf16[272,768]{1,0:T(8,128)(2,1)S(1)}, f32[256,768]{1,0:T(8,128)S(1)}) custom-call(bf16[512,2048]{1,0:T(8,128)(2,1)S(1)} %gather_tokens.1.held_ref, bf16[3584,2048]{1,0:T(8,128)(2,1)S(1)} %get-tuple-element.24.refs_1_.weight_ref, bf16[512,3584]{1,0:T(8,128)(2,1)S(1)} %gather_hidden.1.refs_0_.hidden_ref), custom_call_target="tpu_custom_call" | custom-call | flops 1024 | bytes 1024 | tf_op jit(solution)/shard_map/token_part/pallas_call | solution.py:20
  46.5 0.6 collective-permute-start.12
  47.1 2.0 %token_part.7 = (bf16[272,768]{1,0:T(8,128)(2,1)S(1)}, f32[256,768]{1,0:T(8,128)S(1)}) custom-call(bf16[512,2048]{1,0:T(8,128)(2,1)S(1)} %gather_tokens.1.held_ref, bf16[3584,2048]{1,0:T(8,128)(2,1)S(1)} %get-tuple-element.24.refs_1_.weight_ref, f32[256,768]{1,0:T(8,128)S(1)} %get-tuple-element.27.refs_0_.refs_1_), custom_call_target="tpu_custom_call" | custom-call | flops 1024 | bytes 1024 | tf_op jit(solution)/shard_map/token_part/pallas_call | solution.py:20
  49.1 1.6 %collective-permute-start.11 = (bf16[272,768]{1,0:T(8,128)(2,1)S(1)}, bf16[272,768]{1,0:T(8,128)(2,1)S(1)}, u32[]{:S(2)}, u32[]{:S(2)}) collective-permute-start(bf16[272,768]{1,0:T(8,128)(2,1)S(1)} %get-tuple-element.29), channel_id=1, source_target_pairs={{0,16},{8,24},{16,0},{24,8},{1,17},{9,25},{17,1},{25,9},{2,18},{10... | collective-permute-start | bytes 1253384 | tf_op jit(solution)/shard_map/ppermute | solution.py:82
  50.7 6.8 %weight_part.2 = (bf16[3584,2048]{1,0:T(8,128)(2,1)}, f32[8,128]{1,0:T(8,128)S(1)}) custom-call(bf16[512,2048]{1,0:T(8,128)(2,1)S(1)} %gather_tokens.1.held_ref, bf16[512,3584]{1,0:T(8,128)(2,1)S(1)} %gather_hidden.1.refs_0_.hidden_ref, f32[256,768]{1,0:T(8,128)S(1)} %get-tuple-element.28.refs_0_.refs_1_), custom_call_target="tpu_custom_call" | custom-call | flops 1024 | bytes 1024 | tf_op jit(solution)/shard_map/weight_part/pallas_call | solution.py:20
  57.5 0.0 collective-permute-done.14.refs_0_.refs_1_
  57.6 0.4 combine.4.refs_2_
  58.0 0.6 collective-permute-start.18
  58.5 0.0 collective-permute-done.13.refs_0_.refs_1_
  58.5 0.4 combine.5.refs_2_
  59.0 1.6 %collective-permute-start.17 = (bf16[144,1024]{1,0:T(8,128)(2,1)S(1)}, bf16[144,1024]{1,0:T(8,128)(2,1)S(1)}, u32[]{:S(2)}, u32[]{:S(2)}) collective-permute-start(bf16[144,1024]{1,0:T(8,128)(2,1)S(1)} %combine.5.refs_2_), channel_id=1, source_target_pairs={{0,8},{8,0},{16,24},{24,16},{1,9},{9,1},{17,25},{25,17},{2,10},{10... | collective-permute-start | bytes 884744 | tf_op jit(solution)/shard_map/ppermute | solution.py:82
  60.5 3.4 %collective-permute-done.12.refs_0_.refs_1_ = bf16[272,768]{1,0:T(8,128)(2,1)S(1)} collective-permute-done((bf16[272,768]{1,0:T(8,128)(2,1)S(1)}, bf16[272,768]{1,0:T(8,128)(2,1)S(1)}, u32[]{:S(2)}, u32[]{:S(2)}) %collective-permute-start.12) | collective-permute-done | bytes 417824 | tf_op jit(solution)/shard_map/ppermute | solution.py:82
  63.9 0.3 combine.6.refs_2_
  64.2 1.6 %collective-permute-start.16 = (bf16[144,768]{1,0:T(8,128)(2,1)S(1)}, bf16[144,768]{1,0:T(8,128)(2,1)S(1)}, u32[]{:S(2)}, u32[]{:S(2)}) collective-permute-start(bf16[144,768]{1,0:T(8,128)(2,1)S(1)} %combine.6.refs_2_), channel_id=1, source_target_pairs={{0,16},{8,24},{16,0},{24,8},{1,17},{9,25},{17,1},{25,9},{2,18},{10... | collective-permute-start | bytes 663560 | tf_op jit(solution)/shard_map/ppermute | solution.py:82
  65.8 0.0 collective-permute-done.11.refs_0_.refs_1_
  65.8 0.3 combine.7.refs_0_
  66.1 0.6 collective-permute-start.15
  66.7 6.8 %weight_part.3 = (bf16[3584,2048]{1,0:T(8,128)(2,1)}, f32[8,128]{1,0:T(8,128)S(1)}) custom-call(bf16[512,2048]{1,0:T(8,128)(2,1)S(1)} %gather_tokens.1.held_ref, bf16[512,3584]{1,0:T(8,128)(2,1)S(1)} %gather_hidden.1.refs_0_.hidden_ref, bf16[144,768]{1,0:T(8,128)(2,1)S(1)} %combine.7.refs_0_, ...), custom_call_target="tpu_custom_call", output_to_operand_aliasing={{0}: (3, {})} | custom-call | flops 1024 | bytes 1024 | tf_op jit(solution)/shard_map/weight_part/pallas_call | solution.py:20
  73.5 0.0 collective-permute-done.18.refs_2_
  73.6 1.0 %finish.4 = (bf16[128,3584]{1,0:T(8,128)(2,1)}, f32[8,128]{1,0:T(8,128)S(1)}) custom-call(f32[256,1024]{1,0:T(8,128)S(1)} %get-tuple-element.25.refs_0_.refs_1_, bf16[272,1024]{1,0:T(8,128)(2,1)S(1)} %collective-permute-done.14.refs_0_.refs_1_, bf16[144,1024]{1,0:T(8,128)(2,1)S(1)} %collective-permute-done.18.refs_2_, f32[8,128]{1,0:T(8,128)S(1)} %get-tuple-element.35.refs_3_), custom_call_target="tpu_custom_call" | custom-call | flops 1024 | bytes 1024 | tf_op jit(solution)/shard_map/finish/pallas_call | solution.py:20
  74.6 0.0 collective-permute-done.17.refs_2_
  74.6 1.0 %finish.5 = (bf16[128,3584]{1,0:T(8,128)(2,1)}, f32[8,128]{1,0:T(8,128)S(1)}) custom-call(f32[256,1024]{1,0:T(8,128)S(1)} %get-tuple-element.26.refs_5_.refs_1_.refs_0_, bf16[272,1024]{1,0:T(8,128)(2,1)S(1)} %collective-permute-done.13.refs_0_.refs_1_, bf16[144,1024]{1,0:T(8,128)(2,1)S(1)} %collective-permute-done.17.refs_2_, ...), custom_call_target="tpu_custom_call", output_to_operand_aliasing={{0}: (4, {})} | custom-call | flops 1024 | bytes 1024 | tf_op jit(solution)/shard_map/finish/pallas_call | solution.py:20
  75.7 0.0 collective-permute-done.16.refs_2_
  75.7 0.9 %finish.6 = (bf16[128,3584]{1,0:T(8,128)(2,1)}, f32[8,128]{1,0:T(8,128)S(1)}) custom-call(f32[256,768]{1,0:T(8,128)S(1)} %get-tuple-element.27.refs_0_.refs_1_, bf16[272,768]{1,0:T(8,128)(2,1)S(1)} %collective-permute-done.12.refs_0_.refs_1_, bf16[144,768]{1,0:T(8,128)(2,1)S(1)} %collective-permute-done.16.refs_2_, ...), custom_call_target="tpu_custom_call", output_to_operand_aliasing={{0}: (4, {})} | custom-call | flops 1024 | bytes 1024 | tf_op jit(solution)/shard_map/finish/pallas_call | solution.py:20
  76.6 0.0 collective-permute-done.15.refs_2_
  76.6 1.5 %finish.7 = (bf16[128,3584]{1,0:T(8,128)(2,1)}, f32[8,128]{1,0:T(8,128)}) custom-call(f32[256,768]{1,0:T(8,128)S(1)} %get-tuple-element.28.refs_0_.refs_1_, bf16[272,768]{1,0:T(8,128)(2,1)S(1)} %collective-permute-done.11.refs_0_.refs_1_, bf16[144,768]{1,0:T(8,128)(2,1)S(1)} %collective-permute-done.15.refs_2_, ...), custom_call_target="tpu_custom_call", output_to_operand_aliasing={{0}: (4, {})} | custom-call | flops 1024 | bytes 1024 | tf_op jit(solution)/shard_map/finish/pallas_call | solution.py:20
  (4 shorter events, 0.1 us)
Async XLA Ops:
  0.6 28.2 %collective-permute-start.7 = (bf16[128,3584]{1,0:T(8,128)(2,1)}, bf16[128,3584]{1,0:T(8,128)(2,1)S(1)}, u32[]{:S(2)}, u32[]{:S(2)}) collective-permute-start(bf16[128,3584]{1,0:T(8,128)(2,1)} %refs_0_.3), channel_id=1, source_target_pairs={{0,8},{8,0},{16,24},{24,16},{1,9},{9,1},{17,25},{25,17},{2,10},{10... | collective-permute-start | bytes 2752520 | tf_op jit(solution)/shard_map/ppermute | solution.py:82
  3.6 25.3 %collective-permute-start.8 = (bf16[128,3584]{1,0:T(8,128)(2,1)}, bf16[128,3584]{1,0:T(8,128)(2,1)S(1)}, u32[]{:S(2)}, u32[]{:S(2)}) collective-permute-start(bf16[128,3584]{1,0:T(8,128)(2,1)} %refs_0_.3), channel_id=1, source_target_pairs={{0,16},{8,24},{16,0},{24,8},{1,17},{9,25},{17,1},{25,9},{2,18},{10... | collective-permute-start | bytes 2752520 | tf_op jit(solution)/shard_map/ppermute | solution.py:82
  5.2 12.3 %collective-permute-start.1 = (bf16[64,2048]{1,0:T(8,128)(2,1)}, bf16[64,2048]{1,0:T(8,128)(2,1)S(1)}, u32[]{:S(2)}, u32[]{:S(2)}) collective-permute-start(bf16[64,2048]{1,0:T(8,128)(2,1)} %refs_0_.2), channel_id=1, source_target_pairs={{0,2},{1,3},{2,0},{3,1},{4,6},{5,7},{6,4},{7,5},{8,10},{9,11},{10,... | collective-permute-start | bytes 786440 | tf_op jit(solution)/shard_map/ppermute | solution.py:92
  6.7 21.6 %collective-permute-start.3 = (bf16[64,2048]{1,0:T(8,128)(2,1)}, bf16[64,2048]{1,0:T(8,128)(2,1)S(1)}, u32[]{:S(2)}, u32[]{:S(2)}) collective-permute-start(bf16[64,2048]{1,0:T(8,128)(2,1)} %refs_0_.2), channel_id=1, source_target_pairs={{0,4},{1,5},{2,6},{3,7},{4,0},{5,1},{6,2},{7,3},{8,12},{9,13},{10,... | collective-permute-start | bytes 786440 | tf_op jit(solution)/shard_map/ppermute | solution.py:92
  9.3 19.0 %collective-permute-start.5 = (bf16[64,2048]{1,0:T(8,128)(2,1)}, bf16[64,2048]{1,0:T(8,128)(2,1)S(1)}, u32[]{:S(2)}, u32[]{:S(2)}) collective-permute-start(bf16[64,2048]{1,0:T(8,128)(2,1)} %refs_0_.2), channel_id=1, source_target_pairs={{0,6},{1,7},{2,4},{3,5},{4,2},{5,3},{6,0},{7,1},{8,14},{9,15},{10,... | collective-permute-start | bytes 786440 | tf_op jit(solution)/shard_map/ppermute | solution.py:92
  17.4 12.2 %collective-permute-start = (bf16[64,2048]{1,0:T(8,128)(2,1)}, bf16[64,2048]{1,0:T(8,128)(2,1)S(1)}, u32[]{:S(2)}, u32[]{:S(2)}) collective-permute-start(bf16[64,2048]{1,0:T(8,128)(2,1)} %refs_0_.2), channel_id=1, source_target_pairs={{0,1},{1,0},{2,3},{3,2},{4,5},{5,4},{6,7},{7,6},{8,9},{9,8},{10,11... | collective-permute-start | bytes 786440 | tf_op jit(solution)/shard_map/ppermute | solution.py:96
  28.3 2.3 %copy-start.1 = (bf16[64,2048]{1,0:T(8,128)(2,1)S(1)}, bf16[64,2048]{1,0:T(8,128)(2,1)}, u32[]{:S(2)}) copy-start(bf16[64,2048]{1,0:T(8,128)(2,1)} %refs_0_.2) | copy-start | bytes 786436
  28.3 1.9 %collective-permute-start.4 = (bf16[64,2048]{1,0:T(8,128)(2,1)S(1)}, bf16[64,2048]{1,0:T(8,128)(2,1)S(1)}, u32[]{:S(2)}, u32[]{:S(2)}) collective-permute-start(bf16[64,2048]{1,0:T(8,128)(2,1)S(1)} %relay.2.refs_4_), channel_id=1, source_target_pairs={{0,1},{1,0},{2,3},{3,2},{4,5},{5,4},{6,7},{7,6},{8,9},{9,8},{10,11... | collective-permute-start | bytes 786440 | tf_op jit(solution)/shard_map/ppermute | solution.py:96
  28.3 1.9 %collective-permute-start.6 = (bf16[64,2048]{1,0:T(8,128)(2,1)S(1)}, bf16[64,2048]{1,0:T(8,128)(2,1)S(1)}, u32[]{:S(2)}, u32[]{:S(2)}) collective-permute-start(bf16[64,2048]{1,0:T(8,128)(2,1)S(1)} %relay.3.refs_6_), channel_id=1, source_target_pairs={{0,1},{1,0},{2,3},{3,2},{4,5},{5,4},{6,7},{7,6},{8,9},{9,8},{10,11... | collective-permute-start | bytes 786440 | tf_op jit(solution)/shard_map/ppermute | solution.py:96
  28.8 1.8 %collective-permute-start.2 = (bf16[64,2048]{1,0:T(8,128)(2,1)S(1)}, bf16[64,2048]{1,0:T(8,128)(2,1)S(1)}, u32[]{:S(2)}, u32[]{:S(2)}) collective-permute-start(bf16[64,2048]{1,0:T(8,128)(2,1)S(1)} %get-tuple-element.23.refs_2_), channel_id=1, source_target_pairs={{0,1},{1,0},{2,3},{3,2},{4,5},{5,4},{6,7},{7,6},{8,9},{9,8},{10,11... | collective-permute-start | bytes 786440 | tf_op jit(solution)/shard_map/ppermute | solution.py:96
  29.0 13.4 %collective-permute-start.9 = (bf16[64,3584]{1,0:T(8,128)(2,1)S(1)}, bf16[64,3584]{1,0:T(8,128)(2,1)S(1)}, u32[]{:S(2)}, u32[]{:S(2)}) collective-permute-start(bf16[64,3584]{1,0:T(8,128)(2,1)S(1)} %slice.8), channel_id=1, source_target_pairs={{0,16},{8,24},{16,0},{24,8},{1,17},{9,25},{17,1},{25,9},{2,18},{10... | collective-permute-start | bytes 1376264 | tf_op jit(solution)/shard_map/ppermute | solution.py:82
  29.6 13.4 %collective-permute-start.10 = (bf16[64,3584]{1,0:T(8,128)(2,1)S(1)}, bf16[64,3584]{1,0:T(8,128)(2,1)S(1)}, u32[]{:S(2)}, u32[]{:S(2)}) collective-permute-start(bf16[64,3584]{1,0:T(8,128)(2,1)S(1)} %slice.9), channel_id=1, source_target_pairs={{0,8},{8,0},{16,24},{24,16},{1,9},{9,1},{17,25},{25,17},{2,10},{10... | collective-permute-start | bytes 1376264 | tf_op jit(solution)/shard_map/ppermute | solution.py:82
  30.9 12.2 %copy-start = (bf16[128,3584]{1,0:T(8,128)(2,1)S(1)}, bf16[128,3584]{1,0:T(8,128)(2,1)}, u32[]{:S(2)}) copy-start(bf16[128,3584]{1,0:T(8,128)(2,1)} %refs_0_.3) | copy-start | bytes 2752516
  33.6 24.0 %collective-permute-start.14 = (bf16[272,1024]{1,0:T(8,128)(2,1)S(1)}, bf16[272,1024]{1,0:T(8,128)(2,1)S(1)}, u32[]{:S(2)}, u32[]{:S(2)}) collective-permute-start(bf16[272,1024]{1,0:T(8,128)(2,1)S(1)} %get-tuple-element.32), channel_id=1, source_target_pairs={{0,8},{8,0},{16,24},{24,16},{1,9},{9,1},{17,25},{25,17},{2,10},{10... | collective-permute-start | bytes 1671176 | tf_op jit(solution)/shard_map/ppermute | solution.py:82
  37.6 20.9 %collective-permute-start.13 = (bf16[272,1024]{1,0:T(8,128)(2,1)S(1)}, bf16[272,1024]{1,0:T(8,128)(2,1)S(1)}, u32[]{:S(2)}, u32[]{:S(2)}) collective-permute-start(bf16[272,1024]{1,0:T(8,128)(2,1)S(1)} %get-tuple-element.31), channel_id=1, source_target_pairs={{0,16},{8,24},{16,0},{24,8},{1,17},{9,25},{17,1},{25,9},{2,18},{10... | collective-permute-start | bytes 1671176 | tf_op jit(solution)/shard_map/ppermute | solution.py:82
  46.5 17.4 %collective-permute-start.12 = (bf16[272,768]{1,0:T(8,128)(2,1)S(1)}, bf16[272,768]{1,0:T(8,128)(2,1)S(1)}, u32[]{:S(2)}, u32[]{:S(2)}) collective-permute-start(bf16[272,768]{1,0:T(8,128)(2,1)S(1)} %get-tuple-element.30), channel_id=1, source_target_pairs={{0,8},{8,0},{16,24},{24,16},{1,9},{9,1},{17,25},{25,17},{2,10},{10... | collective-permute-start | bytes 1253384 | tf_op jit(solution)/shard_map/ppermute | solution.py:82
  49.1 16.7 %collective-permute-start.11 = (bf16[272,768]{1,0:T(8,128)(2,1)S(1)}, bf16[272,768]{1,0:T(8,128)(2,1)S(1)}, u32[]{:S(2)}, u32[]{:S(2)}) collective-permute-start(bf16[272,768]{1,0:T(8,128)(2,1)S(1)} %get-tuple-element.29), channel_id=1, source_target_pairs={{0,16},{8,24},{16,0},{24,8},{1,17},{9,25},{17,1},{25,9},{2,18},{10... | collective-permute-start | bytes 1253384 | tf_op jit(solution)/shard_map/ppermute | solution.py:82
  58.0 15.6 %collective-permute-start.18 = (bf16[144,1024]{1,0:T(8,128)(2,1)S(1)}, bf16[144,1024]{1,0:T(8,128)(2,1)S(1)}, u32[]{:S(2)}, u32[]{:S(2)}) collective-permute-start(bf16[144,1024]{1,0:T(8,128)(2,1)S(1)} %combine.4.refs_2_), channel_id=1, source_target_pairs={{0,16},{8,24},{16,0},{24,8},{1,17},{9,25},{17,1},{25,9},{2,18},{10... | collective-permute-start | bytes 884744 | tf_op jit(solution)/shard_map/ppermute | solution.py:82
  59.0 15.7 %collective-permute-start.17 = (bf16[144,1024]{1,0:T(8,128)(2,1)S(1)}, bf16[144,1024]{1,0:T(8,128)(2,1)S(1)}, u32[]{:S(2)}, u32[]{:S(2)}) collective-permute-start(bf16[144,1024]{1,0:T(8,128)(2,1)S(1)} %combine.5.refs_2_), channel_id=1, source_target_pairs={{0,8},{8,0},{16,24},{24,16},{1,9},{9,1},{17,25},{25,17},{2,10},{10... | collective-permute-start | bytes 884744 | tf_op jit(solution)/shard_map/ppermute | solution.py:82
  64.2 11.5 %collective-permute-start.16 = (bf16[144,768]{1,0:T(8,128)(2,1)S(1)}, bf16[144,768]{1,0:T(8,128)(2,1)S(1)}, u32[]{:S(2)}, u32[]{:S(2)}) collective-permute-start(bf16[144,768]{1,0:T(8,128)(2,1)S(1)} %combine.6.refs_2_), channel_id=1, source_target_pairs={{0,16},{8,24},{16,0},{24,8},{1,17},{9,25},{17,1},{25,9},{2,18},{10... | collective-permute-start | bytes 663560 | tf_op jit(solution)/shard_map/ppermute | solution.py:82
  66.1 10.5 %collective-permute-start.15 = (bf16[144,768]{1,0:T(8,128)(2,1)S(1)}, bf16[144,768]{1,0:T(8,128)(2,1)S(1)}, u32[]{:S(2)}, u32[]{:S(2)}) collective-permute-start(bf16[144,768]{1,0:T(8,128)(2,1)S(1)} %combine.7.refs_0_), channel_id=1, source_target_pairs={{0,8},{8,0},{16,24},{24,16},{1,9},{9,1},{17,25},{25,17},{2,10},{10... | collective-permute-start | bytes 663560 | tf_op jit(solution)/shard_map/ppermute | solution.py:82

commit v3 on v2

v3 whole, which is shorter than its diff:
```python
import functools

import jax
import jax.numpy as jnp
from jax import lax
from jax.experimental import pallas as pl
from jax.experimental.pallas import tpu as pltpu
from jax.sharding import PartitionSpec as P

CORES = 2
SPAN = 120.0
SCALE_ROWS = 16
LANES = 128
TILE = 512
FLOPS = 2 * 10**9
SLOTS = 4
COST = 0
SCOPED = 20 * 1024 * 1024
ANY, HBM, VMEM = pl.ANY, pltpu.HBM, pltpu.VMEM
MARK = ((8, 128), jnp.float32, VMEM)


def call(kernel, name, operands, results, scratch=(), aliases={}, flops=0):
    return pl.pallas_call(
        kernel,
        in_specs=[pl.BlockSpec(memory_space=memory) for _, memory in operands],
        out_specs=[pl.BlockSpec(memory_space=memory) for _, _, memory in results],
        out_shape=[
            jax.ShapeDtypeStruct(shape, dtype) if memory is ANY else memory(shape, dtype)
            for shape, dtype, memory in results
        ],
        scratch_shapes=list(scratch),
        input_output_aliases=aliases,
        compiler_params=pltpu.CompilerParams(vmem_limit_bytes=SCOPED),
        cost_estimate=pl.CostEstimate(flops=flops, bytes_accessed=COST, transcendentals=0),
        name=name,
    )(*[pltpu.with_memory_space_constraint(array, memory) for array, memory in operands])


def grid_of(n):
    ny = int(n**0.5)
    while n % ny:
        ny -= 1
    return ny, n // ny


def message_shape(rows, width):
    runs = width // LANES
    return (runs * rows + -(-runs // SCALE_ROWS) * SCALE_ROWS, LANES)


def encode(blocks):
    top = functools.reduce(jnp.maximum, [jnp.max(jnp.abs(block), axis=0, keepdims=True) for block in blocks])
    scale = jnp.maximum(top * 1.0078125, 1e-36).astype(jnp.bfloat16).astype(jnp.float32)
    step = 2 * SPAN / scale
    codes = []
    for block in blocks:
        size = jnp.exp2(jnp.abs(block) * step - SPAN)
        codes.append(jnp.where(block < 0, -size, size).astype(jnp.bfloat16))
    return codes, scale


def store_codes(ref, first, blocks):
    codes, scale = encode(blocks)
    rows = sum(code.shape[0] for code in codes)
    scales = []
    for at in range(0, scale.shape[1], LANES):
        start = (first + at) // LANES * rows
        for code in codes:
            ref[start : start + code.shape[0], :] = code[:, at : at + LANES]
            start += code.shape[0]
        scales.append(scale[:, at : at + LANES])
    return scales


def store_scales(ref, scales):
    extra = -len(scales) % SCALE_ROWS
    full = jnp.concatenate(scales + [jnp.ones((extra, LANES), jnp.float32)] * (extra > 0), axis=0)
    ref[ref.shape[0] - full.shape[0] :, :] = full.astype(jnp.bfloat16)


def decode(ref, group, start, stop, width):
    runs = width // LANES
    scales = ref[runs * group :, :].astype(jnp.float32) * (0.5 / SPAN)
    values = []
    for run in range(runs):
        code = ref[run * group + start : run * group + stop, :].astype(jnp.float32)
        size = (jnp.log2(jnp.abs(code)) + SPAN) * scales[run : run + 1]
        values.append(jnp.where(code < 0, -size, size))
    return values


class Plan:
    def __init__(self, mesh):
        self.n, self.m = mesh.shape["row"], mesh.shape["col"]
        self.ny, self.nx = grid_of(self.n)
        self.nz = self.m // CORES
        self.turned = self.ny == self.nx
        self.n1, self.n2 = self.nx, self.ny

    def place(self):
        row, col = lax.axis_index("row"), lax.axis_index("col")
        return row // self.nx, row % self.nx, col // CORES, col % CORES

    def send_row(self, array, first, second):
        pairs = []
        for y in range(self.ny):
            for x in range(self.nx):
                for col in range(self.m):
                    dy, dx = (first, second) if self.turned and col % CORES % 2 else (second, first)
                    to = (y + dy) % self.ny * self.nx + (x + dx) % self.nx
                    pairs.append(((y * self.nx + x) * self.m + col, to * self.m + col))
        return lax.ppermute(array, ("row", "col"), pairs)

    def peer_z(self, z, d):
        return z ^ d if self.nz & (self.nz - 1) == 0 else (z + d) % self.nz

    def from_z(self, z, d):
        return z ^ d if self.nz & (self.nz - 1) == 0 else (z + self.nz - d) % self.nz

    def direct(self, d):
        return self.nz & (self.nz - 1) != 0 or d & (d - 1) == 0

    def send_z(self, array, d):
        pairs = [(z * CORES + c, self.peer_z(z, d) * CORES + c) for z in range(self.nz) for c in range(CORES)]
        return lax.ppermute(array, "col", pairs)

    def swap(self, array, d):
        pairs = [(z * CORES + c, z * CORES + (c + d) % CORES) for z in range(self.nz) for c in range(CORES)]
        return lax.ppermute(array, "col", pairs)

    def token_copies(self, pieces, held, sems):
        y, x, z, core = self.place()
        rows = pieces[0].shape[0]
        per = self.m // self.n
        copies = []
        for at in range(len(pieces)):
            d, c = at // CORES, at % CORES
            origin = self.from_z(z, d) * CORES + lax.rem(core + CORES - c, CORES)
            owner = origin // per
            dy = lax.rem(owner // self.nx + self.ny - y, self.ny)
            dx = lax.rem(owner % self.nx + self.nx - x, self.nx)
            turn = lax.rem(core, 2) if self.turned else 0
            slot = (dx + turn * (dy - dx)) * self.n2 + dy + turn * (dx - dy)
            start = pl.multiple_of((slot * per + origin % per) * rows, rows)
            copies.append(pltpu.make_async_copy(pieces[at], held.at[pl.ds(start, rows), :], sems.at[at]))
        return copies

    def hold(self, hidden, relay):
        def kernel(hidden_ref, *refs):
            out, _, sem = refs[-3:]
            copy = pltpu.make_async_copy(hidden_ref, out, sem)
            copy.start()
            copy.wait()

        return call(
            kernel,
            "hold",
            [(hidden, HBM), (relay, ANY)],
            [(hidden.shape, hidden.dtype, VMEM), (relay.shape, relay.dtype, ANY)],
            [pltpu.SemaphoreType.DMA],
            aliases={1: 1},
        )

    def stage(self, weight, relay):
        def kernel(weight_ref, *refs):
            out, _, sem = refs[-3:]
            copy = pltpu.make_async_copy(weight_ref, out, sem)
            copy.start()
            copy.wait()

        return call(
            kernel,
            "stage",
            [(weight, HBM), (relay, ANY)],
            [(weight.shape, weight.dtype, VMEM), (relay.shape, relay.dtype, ANY)],
            [pltpu.SemaphoreType.DMA],
            aliases={1: 1},
        )

    def relay(self, arrays, after):
        operands = [(array, ANY) for array in (*arrays, *after)]
        results = [(array.shape, array.dtype, ANY) for array in arrays]
        return list(call(lambda *refs: None, "relay", operands, results, aliases={at: at for at in range(len(arrays))}))

    def gather_tokens(self, pieces, after):
        count, (rows, depth) = len(pieces), pieces[0].shape

        def kernel(*refs):
            out, sems = refs[-2:]
            copies = self.token_copies(refs[:count], out, sems)
            for copy in copies:
                copy.start()
            for copy in copies:
                copy.wait()

        return call(
            kernel,
            "gather_tokens",
            [(piece, ANY) for piece in pieces] + [(array, ANY) for array in after],
            [((count * rows, depth), jnp.bfloat16, VMEM)],
            [pltpu.SemaphoreType.DMA((count,))],
        )[0]

    def token_part(self, held, weight, first, width, after, flops):
        tokens, depth = held.shape
        group = tokens // self.n1
        results = [(message_shape(group, width), jnp.bfloat16, VMEM)] * (self.n1 - 1) + [((group, width), jnp.float32, VMEM)]

        def kernel(held_ref, weight_ref, *refs):
            outs = refs[len(after) :]
            messages, keep = outs[:-1], outs[-1]
            scales = [[] for _ in messages]
            for at in range(0, width, TILE):
                size = min(TILE, width - at)
                total = lax.dot_general(
                    held_ref[...],
                    weight_ref[first + at : first + at + size, :],
                    (((1,), (1,)), ((), ())),
                    preferred_element_type=jnp.float32,
                )
                keep[:, at : at + size] = total[:group]
                for peer in range(1, self.n1):
                    scales[peer - 1] += store_codes(messages[peer - 1], at, [total[peer * group : (peer + 1) * group]])
            for message, rows in zip(messages, scales):
                store_scales(message, rows)

        operands = [(array, VMEM) for array in (held, weight, *after)]
        *messages, keep = call(kernel, "token_part", operands, results, flops=flops)
        return messages, keep

    def combine(self, got, keep, after):
        group, width = keep.shape
        own = group // self.n2
        operands = [(array, VMEM) for array in (*got, keep, *after)]

        def kernel(*refs):
            messages, keep_ref, outs = refs[: len(got)], refs[len(got)], refs[len(operands) :]
            for block in range(1, self.n2):
                start, stop = block * own, (block + 1) * own
                brought = [decode(message, group, start, stop, width) for message in messages]
                scales = []
                for run in range(width // LANES):
                    at = run * LANES
                    total = keep_ref[start:stop, at : at + LANES]
                    for values in brought:
                        total = total + values[run]
                    scales += store_codes(outs[block - 1], at, [total])
                store_scales(outs[block - 1], scales)

        return list(call(kernel, "combine", operands, [(message_shape(own, width), jnp.bfloat16, VMEM)] * (self.n2 - 1)))

    def finish(self, parts, lates, own, units, so_far, after):
        operands, scratch = [], []
        for (_, got, keep), late in zip(parts, lates):
            scratch.append(pltpu.VMEM((own, keep.shape[1]), jnp.bfloat16))
            operands += [(array, VMEM) for array in (keep, *got, *late)]
        extra = [(so_far, HBM)] if so_far is not None else []

        def kernel(*refs):
            out, _, *bufs, sems = refs[len(operands) + len(after) + len(extra) :]
            copies = []
            for index, ((first, got, keep), late) in enumerate(zip(parts, lates)):
                width = keep.shape[1]
                keep_ref, firsts = refs[0], refs[1 : 1 + len(got)]
                seconds = refs[1 + len(got) : 1 + len(got) + len(late)]
                refs = refs[1 + len(got) + len(late) :]
                brought = [decode(message, keep.shape[0], 0, own, width) for message in firsts]
                brought += [decode(message, own, 0, own, width) for message in seconds]
                for run in range(width // LANES):
                    columns = slice(run * LANES, (run + 1) * LANES)
                    total = keep_ref[:own, columns]
                    for values in brought:
                        total = total + values[run]
                    bufs[index][:, columns] = total.astype(jnp.bfloat16)
                copies.append(pltpu.make_async_copy(bufs[index], out.at[:, pl.ds(first, width)], sems.at[index]))
                copies[-1].start()
            for copy in copies:
                copy.wait()

        return call(
            kernel,
            "finish",
            operands + [(array, VMEM) for array in after] + extra,
            [((own, units), jnp.bfloat16, HBM), MARK],
            scratch + [pltpu.SemaphoreType.DMA((len(parts),))],
            aliases={len(operands) + len(after): 0} if extra else {},
        )

    def weight_part(self, held, blocks, first, width, tile, so_far, after):
        depth, units = held.shape[1], blocks[0].shape[1]
        steps = width // tile
        extra = [(so_far, HBM)] if so_far is not None else []
        operands = [(array, VMEM) for array in (held, *blocks, *after)]

        def kernel(held_ref, *refs):
            out, _, buf, sems = refs[-4:]
            pending = []
            for s in range(steps):
                if s >= SLOTS:
                    pending[s - SLOTS].wait()
                start = first + s * tile
                buf[s % SLOTS] = lax.dot_general(
                    jnp.concatenate([ref[:, start : start + tile] for ref in refs[: len(blocks)]], axis=0),
                    held_ref[...],
                    (((0,), (0,)), ((), ())),
                    preferred_element_type=jnp.float32,
                ).astype(jnp.bfloat16)
                pending.append(pltpu.make_async_copy(buf.at[s % SLOTS], out.at[pl.ds(start, tile), :], sems.at[s % SLOTS]))
                pending[-1].start()
            for copy in pending[-SLOTS:]:
                copy.wait()

        return call(
            kernel,
            "weight_part",
            operands + extra,
            [((units, depth), jnp.bfloat16, HBM), MARK],
            [pltpu.VMEM((SLOTS, tile, depth), jnp.bfloat16), pltpu.SemaphoreType.DMA((SLOTS,))],
            aliases={len(operands): 0} if extra else {},
        )


def cut(tiles, shares):
    ends = [round(tiles * sum(shares[: at + 1]) / sum(shares)) for at in range(len(shares))]
    return [(start, end) for start, end in zip([0, *ends], ends) if end > start]


def on_device(plan, out_grad, hidden, weight):
    n1, n2 = plan.n1, plan.n2
    own, units = hidden.shape
    near = [plan.send_row(hidden, s, 0) for s in range(1, n1)]
    far = {d: plan.send_z(out_grad, d) for d in range(1, plan.nz) if plan.direct(d)}
    swapped = [plan.swap(out_grad, c) for c in range(1, CORES)]
    hidden, swapped[0] = plan.hold(hidden, swapped[0])
    side = [plan.send_row(hidden, 0, s) for s in range(1, n2)]
    weight, swapped[0] = plan.stage(weight, swapped[0])
    far[1] = plan.relay([far[1]], [weight])[0]
    near = plan.relay(near, [far[1]])
    later = [d for d in far if d > 1]
    far.update(zip(later, plan.relay([far[d] for d in later], near)))
    pieces = [out_grad] + swapped
    for d in range(1, plan.nz):
        if d not in far:
            far[d] = plan.send_z(far[d & (d - 1)], d & -d)
        pieces += [far[d]] + [plan.swap(far[d], c) for c in range(1, CORES)]

    passed = [[plan.send_row(piece, 0, s) for s in range(1, n2)] for piece in near]
    came = [[hidden] + side] + [[piece] + on for piece, on in zip(near, passed)]
    blocks = [came[-e1 % n1][-e2 % n2] for e1 in range(n1) for e2 in range(n2)]

    tile = 256 if units % 256 == 0 else 128
    rounds = [(start * tile, (end - start) * tile) for start, end in cut(units // tile, ROUNDS)]
    runs = [(start * tile, (end - start) * tile) for start, end in cut(units // tile, RUNS)]

    weight_grad = token_grad = None
    held = plan.gather_tokens(pieces, [])
    last, parts, lates = [], [], []

    def part(at):
        nonlocal last
        messages, keep = plan.token_part(held, weight, *rounds[at], last, FLOPS if at <= WAIT else 0)
        last = [keep]
        if at == min(WAIT, len(rounds) - 1):
            messages = plan.relay(messages, sum(passed, []) + side)
        parts.append((rounds[at][0], [plan.send_row(m, s + 1, 0) for s, m in enumerate(messages)], keep))

    def join(at):
        nonlocal last
        onward = plan.combine(parts[at][1], parts[at][2], last)
        last = onward[:1]
        lates.append([plan.send_row(m, 0, s + 1) for s, m in enumerate(onward)])

    def weigh(at):
        nonlocal last, weight_grad
        weight_grad, mark = plan.weight_part(held, blocks, *runs[at], tile, weight_grad, last)
        last = [mark]

    def end(start, stop):
        nonlocal last, token_grad
        token_grad, mark = plan.finish(parts[start:stop], lates[start:stop], own, units, token_grad, last)
        last = [mark]

    for name, at in PROGRAM:
        if name == "part" and at < len(rounds):
            part(at)
        elif name == "join" and at < len(rounds):
            join(at)
        elif name == "weigh" and at < len(runs):
            weigh(at)
        elif name == "end" and at < len(rounds):
            end(at, min(at + ENDS, len(rounds)))
    return token_grad, weight_grad


ROUNDS = (4, 4, 4, 2)
RUNS = (7, 4, 3)
ENDS = 2
WAIT = 1
PROGRAM = [
    ("part", 0),
    ("part", 1),
    ("part", 2),
    ("part", 3),
    ("weigh", 0),
    ("join", 0),
    ("join", 1),
    ("weigh", 1),
    ("join", 2),
    ("join", 3),
    ("end", 0),
    ("weigh", 2),
    ("end", 2),
]


def solution(mesh):
    return jax.shard_map(
        functools.partial(on_device, Plan(mesh)),
        mesh=mesh,
        in_specs=(P("col", "row"), P("row", "col"), P("col", "row")),
        out_specs=(P("row", "col"), P("col", "row")),
        check_vma=False,
    )
```

time: 79.6 us -> 69.8 us (0.88)
  waiting for transfers between devices: 21.3 us -> 12.7 us
  Pallas kernels: 36 us -> 32.7 us
  starting transfers between devices: 20 us -> 22.1 us
    ppermute x3, waiting for transfers between devices: 13.6 us -> 6.07 us  [send_z(): return lax.ppermute(array, 'col', pairs)]
    pallas_call x19 -> x20, Pallas kernels: 36 us -> 32.7 us  [call(): pl.pallas_call(kernel, in_specs=[pl.BlockSpec(memory_space=memory) for _,...]
    ppermute x3, starting transfers between devices: 4.39 us -> 6.87 us  [send_z(): return lax.ppermute(array, 'col', pairs)]
    ppermute x12 -> x11, waiting for transfers between devices: 7.24 us -> 5.07 us  [send_row(): return lax.ppermute(array, ('row', 'col'), pairs)]
    ppermute x4, waiting for transfers between devices: 0.43 us -> 1.53 us  [swap(): return lax.ppermute(array, 'col', pairs)]
    ppermute x12 -> x11, starting transfers between devices: 15.1 us -> 14.7 us  [send_row(): return lax.ppermute(array, ('row', 'col'), pairs)]
  transfers between devices with their start and end apart: 19 -> 18, of which waited for: 6 -> 5; matrix products, arithmetic and copies ran while one was open for 0% -> 0% of each run, Pallas kernels for 44% -> 45%
where the time goes in v3:
time: 69.8 us; the launch traced here: 68.4 us
  Pallas kernels  32.7 us (47%)
  starting transfers between devices  22.1 us (32%)
  waiting for transfers between devices  12.7 us (18%)
  between operations  0.98 us (1%)
    pallas_call x20, Pallas kernels, call(): pl.pallas_call(kernel, in_specs=[pl.BlockSpec(memory_space=memory) for _,...  32.7 us
    ppermute x11, starting transfers between devices, send_row(): return lax.ppermute(array, ('row', 'col'), pairs)  14.7 us
    ppermute x3, starting transfers between devices, send_z(): return lax.ppermute(array, 'col', pairs)  6.87 us
    ppermute x3, waiting for transfers between devices, send_z(): return lax.ppermute(array, 'col', pairs)  6.07 us
    ppermute x11, waiting for transfers between devices, send_row(): return lax.ppermute(array, ('row', 'col'), pairs)  5.07 us
    ppermute x4, waiting for transfers between devices, swap(): return lax.ppermute(array, 'col', pairs)  1.53 us
  transfers between devices with their start and end apart: 18, of which 5 were waited for; matrix products, arithmetic and copies ran while one was open for 0% of the time, Pallas kernels for 45%

profile of v3, /device:TPU:0, one launch (start us, length us, event | category | flops | bytes accessed | tf_op | source)
XLA Modules:
  0.0 68.4 jit_solution(9829902961595484818)
XLA Ops:
  0.6 3.0 %collective-permute-start.4 = (bf16[128,3584]{1,0:T(8,128)(2,1)}, bf16[128,3584]{1,0:T(8,128)(2,1)S(1)}, u32[]{:S(2)}, u32[]{:S(2)}) collective-permute-start(bf16[128,3584]{1,0:T(8,128)(2,1)} %hidden_ref.1), channel_id=1, source_target_pairs={{0,8},{1,17},{2,10},{3,19},{4,12},{5,21},{6,14},{7,23},{8,0},{9,25... | collective-permute-start | bytes 2752520 | tf_op jit(solution)/shard_map/ppermute | solution.py:113
  3.6 0.0 collective-permute-start
  3.6 1.6 %collective-permute-start.1 = (bf16[64,2048]{1,0:T(8,128)(2,1)}, bf16[64,2048]{1,0:T(8,128)(2,1)S(1)}, u32[]{:S(2)}, u32[]{:S(2)}) collective-permute-start(bf16[64,2048]{1,0:T(8,128)(2,1)} %refs_0_.1), channel_id=1, source_target_pairs={{0,2},{1,3},{2,0},{3,1},{4,6},{5,7},{6,4},{7,5},{8,10},{9,11},{10,... | collective-permute-start | bytes 786440 | tf_op jit(solution)/shard_map/ppermute | solution.py:126
  5.2 2.6 %collective-permute-start.3 = (bf16[64,2048]{1,0:T(8,128)(2,1)}, bf16[64,2048]{1,0:T(8,128)(2,1)S(1)}, u32[]{:S(2)}, u32[]{:S(2)}) collective-permute-start(bf16[64,2048]{1,0:T(8,128)(2,1)} %refs_0_.1), channel_id=1, source_target_pairs={{0,4},{1,5},{2,6},{3,7},{4,0},{5,1},{6,2},{7,3},{8,12},{9,13},{10,... | collective-permute-start | bytes 786440 | tf_op jit(solution)/shard_map/ppermute | solution.py:126
  7.8 0.0 collective-permute-done.refs_0_
  7.8 1.2 %hold.1 = (bf16[128,3584]{1,0:T(8,128)(2,1)S(1)}, bf16[64,2048]{1,0:T(8,128)(2,1)S(1)}) custom-call(bf16[128,3584]{1,0:T(8,128)(2,1)} %hidden_ref.1, bf16[64,2048]{1,0:T(8,128)(2,1)S(1)} %collective-permute-done.refs_0_), custom_call_target="tpu_custom_call", output_to_operand_aliasing={{1}: (1, {})} | custom-call | tf_op jit(solution)/shard_map/hold/pallas_call | solution.py:24
  9.0 1.6 %collective-permute-start.9 = (bf16[128,3584]{1,0:T(8,128)(2,1)S(1)}, bf16[128,3584]{1,0:T(8,128)(2,1)S(1)}, u32[]{:S(2)}, u32[]{:S(2)}) collective-permute-start(bf16[128,3584]{1,0:T(8,128)(2,1)S(1)} %get-tuple-element.30.refs_0_), channel_id=1, source_target_pairs={{0,16},{1,9},{2,18},{3,11},{4,20},{5,13},{6,22},{7,15},{8,24},{9,1... | collective-permute-start | bytes 2752520 | tf_op jit(solution)/shard_map/ppermute | solution.py:113
  10.6 0.0 copy-start
  10.6 5.2 %stage.1 = (bf16[3584,2048]{1,0:T(8,128)(2,1)S(1)}, bf16[64,2048]{1,0:T(8,128)(2,1)S(1)}) custom-call(bf16[3584,2048]{1,0:T(8,128)(2,1)} %weight_ref.1, bf16[64,2048]{1,0:T(8,128)(2,1)S(1)} %get-tuple-element.23.refs_0_), custom_call_target="tpu_custom_call", output_to_operand_aliasing={{1}: (1, {})} | custom-call | tf_op jit(solution)/shard_map/stage/pallas_call | solution.py:24
  15.8 2.2 %collective-permute-done.1.refs_0_ = bf16[64,2048]{1,0:T(8,128)(2,1)S(1)} collective-permute-done((bf16[64,2048]{1,0:T(8,128)(2,1)}, bf16[64,2048]{1,0:T(8,128)(2,1)S(1)}, u32[]{:S(2)}, u32[]{:S(2)}) %collective-permute-start.1) | collective-permute-done | bytes 262176 | tf_op jit(solution)/shard_map/ppermute | solution.py:126
  18.1 1.8 %collective-permute-done.4.refs_0_ = bf16[128,3584]{1,0:T(8,128)(2,1)S(1)} collective-permute-done((bf16[128,3584]{1,0:T(8,128)(2,1)}, bf16[128,3584]{1,0:T(8,128)(2,1)S(1)}, u32[]{:S(2)}, u32[]{:S(2)}) %collective-permute-start.4) | collective-permute-done | bytes 917536 | tf_op jit(solution)/shard_map/ppermute | solution.py:113
  19.9 1.6 %collective-permute-start.10 = (bf16[128,3584]{1,0:T(8,128)(2,1)S(1)}, bf16[128,3584]{1,0:T(8,128)(2,1)S(1)}, u32[]{:S(2)}, u32[]{:S(2)}) collective-permute-start(bf16[128,3584]{1,0:T(8,128)(2,1)S(1)} %relay.5.refs_1_.refs_2_), channel_id=1, source_target_pairs={{0,16},{1,9},{2,18},{3,11},{4,20},{5,13},{6,22},{7,15},{8,24},{9,1... | collective-permute-start | bytes 2752520 | tf_op jit(solution)/shard_map/ppermute | solution.py:113
  21.4 0.0 collective-permute-done.3.refs_0_
  21.4 2.7 %collective-permute-start.6 = (bf16[64,2048]{1,0:T(8,128)(2,1)S(1)}, bf16[64,2048]{1,0:T(8,128)(2,1)S(1)}, u32[]{:S(2)}, u32[]{:S(2)}) collective-permute-start(bf16[64,2048]{1,0:T(8,128)(2,1)S(1)} %relay.6.refs_4_), channel_id=1, source_target_pairs={{0,2},{1,3},{2,0},{3,1},{4,6},{5,7},{6,4},{7,5},{8,10},{9,11},{10,... | collective-permute-start | bytes 786440 | tf_op jit(solution)/shard_map/ppermute | solution.py:126
  24.1 0.0 collective-permute-start.2
  24.1 0.5 collective-permute-start.5
  24.6 3.8 %collective-permute-done.6.refs_6_ = bf16[64,2048]{1,0:T(8,128)(2,1)S(1)} collective-permute-done((bf16[64,2048]{1,0:T(8,128)(2,1)S(1)}, bf16[64,2048]{1,0:T(8,128)(2,1)S(1)}, u32[]{:S(2)}, u32[]{:S(2)}) %collective-permute-start.6) | collective-permute-done | bytes 262176 | tf_op jit(solution)/shard_map/ppermute | solution.py:126
  28.5 0.0 collective-permute-start.7
  28.5 0.0 collective-permute-done.2.refs_3_
  28.5 0.0 collective-permute-done.5.refs_5_
  28.5 1.5 %collective-permute-done.7.refs_7_ = bf16[64,2048]{1,0:T(8,128)(2,1)S(1)} collective-permute-done((bf16[64,2048]{1,0:T(8,128)(2,1)S(1)}, bf16[64,2048]{1,0:T(8,128)(2,1)S(1)}, u32[]{:S(2)}, u32[]{:S(2)}) %collective-permute-start.7) | collective-permute-done | bytes 262176 | tf_op jit(solution)/shard_map/ppermute | solution.py:130
  30.0 0.0 copy-done
  30.0 0.3 gather_tokens.1.held_ref
  30.3 2.7 %token_part.4 = (bf16[2064,128]{1,0:T(8,128)(2,1)S(1)}, f32[256,1024]{1,0:T(8,128)S(1)}) custom-call(bf16[512,2048]{1,0:T(8,128)(2,1)S(1)} %gather_tokens.1.held_ref, bf16[3584,2048]{1,0:T(8,128)(2,1)S(1)} %get-tuple-element.25.refs_1_.weight_ref), custom_call_target="tpu_custom_call" | custom-call | flops 2000000000 | tf_op jit(solution)/shard_map/token_part/pallas_call | solution.py:24
  33.0 2.4 %collective-permute-start.12 = (bf16[2064,128]{1,0:T(8,128)(2,1)S(1)}, bf16[2064,128]{1,0:T(8,128)(2,1)S(1)}, u32[]{:S(2)}, u32[]{:S(2)}) collective-permute-start(bf16[2064,128]{1,0:T(8,128)(2,1)S(1)} %get-tuple-element.32), channel_id=1, source_target_pairs={{0,8},{1,17},{2,10},{3,19},{4,12},{5,21},{6,14},{7,23},{8,0},{9,25... | collective-permute-start | bytes 1585160 | tf_op jit(solution)/shard_map/ppermute | solution.py:113
  35.4 2.7 %token_part.5 = (bf16[2064,128]{1,0:T(8,128)(2,1)S(1)}, f32[256,1024]{1,0:T(8,128)S(1)}) custom-call(bf16[512,2048]{1,0:T(8,128)(2,1)S(1)} %gather_tokens.1.held_ref, bf16[3584,2048]{1,0:T(8,128)(2,1)S(1)} %get-tuple-element.25.refs_1_.weight_ref, f32[256,1024]{1,0:T(8,128)S(1)} %get-tuple-element.26.refs_0_.refs_1_), custom_call_target="tpu_custom_call" | custom-call | flops 2000000000 | tf_op jit(solution)/shard_map/token_part/pallas_call | solution.py:24
  38.1 0.0 collective-permute-done.9.refs_2_.refs_1_
  38.1 0.0 collective-permute-done.10.refs_1_.refs_3_
  38.1 0.1 collective-permute-start.11
  38.2 2.7 %token_part.6 = (bf16[2064,128]{1,0:T(8,128)(2,1)S(1)}, f32[256,1024]{1,0:T(8,128)S(1)}) custom-call(bf16[512,2048]{1,0:T(8,128)(2,1)S(1)} %gather_tokens.1.held_ref, bf16[3584,2048]{1,0:T(8,128)(2,1)S(1)} %get-tuple-element.25.refs_1_.weight_ref, f32[256,1024]{1,0:T(8,128)S(1)} %get-tuple-element.27.refs_0_.refs_1_.refs_3_), custom_call_target="tpu_custom_call" | custom-call | tf_op jit(solution)/shard_map/token_part/pallas_call | solution.py:24
  40.9 2.1 %collective-permute-start.8 = (bf16[2064,128]{1,0:T(8,128)(2,1)S(1)}, bf16[2064,128]{1,0:T(8,128)(2,1)S(1)}, u32[]{:S(2)}, u32[]{:S(2)}) collective-permute-start(bf16[2064,128]{1,0:T(8,128)(2,1)S(1)} %get-tuple-element.29), channel_id=1, source_target_pairs={{0,8},{1,17},{2,10},{3,19},{4,12},{5,21},{6,14},{7,23},{8,0},{9,25... | collective-permute-start | bytes 1585160 | tf_op jit(solution)/shard_map/ppermute | solution.py:113
  42.9 1.4 %token_part.7 = (bf16[1040,128]{1,0:T(8,128)(2,1)S(1)}, f32[256,512]{1,0:T(8,128)S(1)}) custom-call(bf16[512,2048]{1,0:T(8,128)(2,1)S(1)} %gather_tokens.1.held_ref, bf16[3584,2048]{1,0:T(8,128)(2,1)S(1)} %get-tuple-element.25.refs_1_.weight_ref, f32[256,1024]{1,0:T(8,128)S(1)} %get-tuple-element.28.refs_0_.refs_1_), custom_call_target="tpu_custom_call" | custom-call | tf_op jit(solution)/shard_map/token_part/pallas_call | solution.py:24
  44.4 0.1 collective-permute-start.14
  44.5 5.7 %weight_part.3 = (bf16[3584,2048]{1,0:T(8,128)(2,1)}, f32[8,128]{1,0:T(8,128)S(1)}) custom-call(bf16[512,2048]{1,0:T(8,128)(2,1)S(1)} %gather_tokens.1.held_ref, bf16[128,3584]{1,0:T(8,128)(2,1)S(1)} %get-tuple-element.30.refs_0_, bf16[128,3584]{1,0:T(8,128)(2,1)S(1)} %collective-permute-done.9.refs_2_.refs_1_, bf16[128,3584]{1,0:T(8,128)(2,1)S(1)} %relay.5.refs_1_.refs_2_, ...), custom_call_target="tpu_custom_call" | custom-call | tf_op jit(solution)/shard_map/weight_part/pallas_call | solution.py:24
  50.1 0.0 collective-permute-done.12.refs_0_.refs_1_
  50.2 0.4 combine.4.refs_2_
  50.5 0.8 %collective-permute-start.16 = (bf16[1040,128]{1,0:T(8,128)(2,1)S(1)}, bf16[1040,128]{1,0:T(8,128)(2,1)S(1)}, u32[]{:S(2)}, u32[]{:S(2)}) collective-permute-start(bf16[1040,128]{1,0:T(8,128)(2,1)S(1)} %combine.4.refs_2_), channel_id=1, source_target_pairs={{0,16},{1,9},{2,18},{3,11},{4,20},{5,13},{6,22},{7,15},{8,24},{9,1... | collective-permute-start | bytes 798728 | tf_op jit(solution)/shard_map/ppermute | solution.py:113
  51.3 0.0 collective-permute-done.11.refs_0_.refs_4_
  51.3 0.4 combine.5.refs_4_
  51.6 1.4 %collective-permute-start.17 = (bf16[1040,128]{1,0:T(8,128)(2,1)S(1)}, bf16[1040,128]{1,0:T(8,128)(2,1)S(1)}, u32[]{:S(2)}, u32[]{:S(2)}) collective-permute-start(bf16[1040,128]{1,0:T(8,128)(2,1)S(1)} %combine.5.refs_4_), channel_id=1, source_target_pairs={{0,16},{1,9},{2,18},{3,11},{4,20},{5,13},{6,22},{7,15},{8,24},{9,1... | collective-permute-start | bytes 798728 | tf_op jit(solution)/shard_map/ppermute | solution.py:113
  53.0 3.6 %weight_part.4 = (bf16[3584,2048]{1,0:T(8,128)(2,1)}, f32[8,128]{1,0:T(8,128)S(1)}) custom-call(bf16[512,2048]{1,0:T(8,128)(2,1)S(1)} %gather_tokens.1.held_ref, bf16[128,3584]{1,0:T(8,128)(2,1)S(1)} %get-tuple-element.30.refs_0_, bf16[128,3584]{1,0:T(8,128)(2,1)S(1)} %collective-permute-done.9.refs_2_.refs_1_, ...), custom_call_target="tpu_custom_call", output_to_operand_aliasing={{0}: (6, {})} | custom-call | tf_op jit(solution)/shard_map/weight_part/pallas_call | solution.py:24
  56.6 0.0 collective-permute-done.8.refs_0_.refs_1_
  56.7 0.4 combine.6.refs_2_
  57.0 0.7 %collective-permute-start.13 = (bf16[1040,128]{1,0:T(8,128)(2,1)S(1)}, bf16[1040,128]{1,0:T(8,128)(2,1)S(1)}, u32[]{:S(2)}, u32[]{:S(2)}) collective-permute-start(bf16[1040,128]{1,0:T(8,128)(2,1)S(1)} %combine.6.refs_2_), channel_id=1, source_target_pairs={{0,16},{1,9},{2,18},{3,11},{4,20},{5,13},{6,22},{7,15},{8,24},{9,1... | collective-permute-start | bytes 798728 | tf_op jit(solution)/shard_map/ppermute | solution.py:113
  57.8 3.2 %collective-permute-done.14.refs_0_.refs_4_ = bf16[1040,128]{1,0:T(8,128)(2,1)S(1)} collective-permute-done((bf16[1040,128]{1,0:T(8,128)(2,1)S(1)}, bf16[1040,128]{1,0:T(8,128)(2,1)S(1)}, u32[]{:S(2)}, u32[]{:S(2)}) %collective-permute-start.14) | collective-permute-done | bytes 266272 | tf_op jit(solution)/shard_map/ppermute | solution.py:113
  61.0 0.2 combine.7.refs_6_
  61.2 1.0 %collective-permute-start.15 = (bf16[528,128]{1,0:T(8,128)(2,1)S(1)}, bf16[528,128]{1,0:T(8,128)(2,1)S(1)}, u32[]{:S(2)}, u32[]{:S(2)}) collective-permute-start(bf16[528,128]{1,0:T(8,128)(2,1)S(1)} %combine.7.refs_6_), channel_id=1, source_target_pairs={{0,16},{1,9},{2,18},{3,11},{4,20},{5,13},{6,22},{7,15},{8,24},{9,1... | collective-permute-start | bytes 405512 | tf_op jit(solution)/shard_map/ppermute | solution.py:113
  62.2 0.0 collective-permute-done.16.refs_2_
  62.2 0.0 collective-permute-done.17.refs_5_
  62.2 1.4 %finish.2 = (bf16[128,3584]{1,0:T(8,128)(2,1)}, f32[8,128]{1,0:T(8,128)S(1)}) custom-call(f32[256,1024]{1,0:T(8,128)S(1)} %get-tuple-element.26.refs_0_.refs_1_, bf16[2064,128]{1,0:T(8,128)(2,1)S(1)} %collective-permute-done.12.refs_0_.refs_1_, bf16[1040,128]{1,0:T(8,128)(2,1)S(1)} %collective-permute-done.16.refs_2_, ...), custom_call_target="tpu_custom_call" | custom-call | tf_op jit(solution)/shard_map/finish/pallas_call | solution.py:24
  63.6 2.9 %weight_part.5 = (bf16[3584,2048]{1,0:T(8,128)(2,1)}, f32[8,128]{1,0:T(8,128)S(1)}) custom-call(bf16[512,2048]{1,0:T(8,128)(2,1)S(1)} %gather_tokens.1.held_ref, bf16[128,3584]{1,0:T(8,128)(2,1)S(1)} %get-tuple-element.30.refs_0_, bf16[128,3584]{1,0:T(8,128)(2,1)S(1)} %collective-permute-done.9.refs_2_.refs_1_, ...), custom_call_target="tpu_custom_call", output_to_operand_aliasing={{0}: (6, {})} | custom-call | tf_op jit(solution)/shard_map/weight_part/pallas_call | solution.py:24
  66.4 0.0 collective-permute-done.15.refs_5_
  66.4 0.0 collective-permute-done.13.refs_2_
  66.5 1.8 %finish.3 = (bf16[128,3584]{1,0:T(8,128)(2,1)}, f32[8,128]{1,0:T(8,128)}) custom-call(f32[256,1024]{1,0:T(8,128)S(1)} %get-tuple-element.28.refs_0_.refs_1_, bf16[2064,128]{1,0:T(8,128)(2,1)S(1)} %collective-permute-done.8.refs_0_.refs_1_, bf16[1040,128]{1,0:T(8,128)(2,1)S(1)} %collective-permute-done.13.refs_2_, ...), custom_call_target="tpu_custom_call", output_to_operand_aliasing={{0}: (7, {})} | custom-call | tf_op jit(solution)/shard_map/finish/pallas_call | solution.py:24
  (4 shorter events, 0.0 us)
Async XLA Ops:
  0.6 19.2 %collective-permute-start.4 = (bf16[128,3584]{1,0:T(8,128)(2,1)}, bf16[128,3584]{1,0:T(8,128)(2,1)S(1)}, u32[]{:S(2)}, u32[]{:S(2)}) collective-permute-start(bf16[128,3584]{1,0:T(8,128)(2,1)} %hidden_ref.1), channel_id=1, source_target_pairs={{0,8},{1,17},{2,10},{3,19},{4,12},{5,21},{6,14},{7,23},{8,0},{9,25... | collective-permute-start | bytes 2752520 | tf_op jit(solution)/shard_map/ppermute | solution.py:113
  3.6 4.2 %collective-permute-start = (bf16[64,2048]{1,0:T(8,128)(2,1)}, bf16[64,2048]{1,0:T(8,128)(2,1)S(1)}, u32[]{:S(2)}, u32[]{:S(2)}) collective-permute-start(bf16[64,2048]{1,0:T(8,128)(2,1)} %refs_0_.1), channel_id=1, source_target_pairs={{0,1},{1,0},{2,3},{3,2},{4,5},{5,4},{6,7},{7,6},{8,9},{9,8},{10,11... | collective-permute-start | bytes 786440 | tf_op jit(solution)/shard_map/ppermute | solution.py:130
  3.6 14.4 %collective-permute-start.1 = (bf16[64,2048]{1,0:T(8,128)(2,1)}, bf16[64,2048]{1,0:T(8,128)(2,1)S(1)}, u32[]{:S(2)}, u32[]{:S(2)}) collective-permute-start(bf16[64,2048]{1,0:T(8,128)(2,1)} %refs_0_.1), channel_id=1, source_target_pairs={{0,2},{1,3},{2,0},{3,1},{4,6},{5,7},{6,4},{7,5},{8,10},{9,11},{10,... | collective-permute-start | bytes 786440 | tf_op jit(solution)/shard_map/ppermute | solution.py:126
  5.2 16.2 %collective-permute-start.3 = (bf16[64,2048]{1,0:T(8,128)(2,1)}, bf16[64,2048]{1,0:T(8,128)(2,1)S(1)}, u32[]{:S(2)}, u32[]{:S(2)}) collective-permute-start(bf16[64,2048]{1,0:T(8,128)(2,1)} %refs_0_.1), channel_id=1, source_target_pairs={{0,4},{1,5},{2,6},{3,7},{4,0},{5,1},{6,2},{7,3},{8,12},{9,13},{10,... | collective-permute-start | bytes 786440 | tf_op jit(solution)/shard_map/ppermute | solution.py:126
  9.0 29.1 %collective-permute-start.9 = (bf16[128,3584]{1,0:T(8,128)(2,1)S(1)}, bf16[128,3584]{1,0:T(8,128)(2,1)S(1)}, u32[]{:S(2)}, u32[]{:S(2)}) collective-permute-start(bf16[128,3584]{1,0:T(8,128)(2,1)S(1)} %get-tuple-element.30.refs_0_), channel_id=1, source_target_pairs={{0,16},{1,9},{2,18},{3,11},{4,20},{5,13},{6,22},{7,15},{8,24},{9,1... | collective-permute-start | bytes 2752520 | tf_op jit(solution)/shard_map/ppermute | solution.py:113
  10.6 19.4 %copy-start = (bf16[64,2048]{1,0:T(8,128)(2,1)S(1)}, bf16[64,2048]{1,0:T(8,128)(2,1)}, u32[]{:S(2)}) copy-start(bf16[64,2048]{1,0:T(8,128)(2,1)} %refs_0_.1) | copy-start | bytes 786436
  19.9 18.2 %collective-permute-start.10 = (bf16[128,3584]{1,0:T(8,128)(2,1)S(1)}, bf16[128,3584]{1,0:T(8,128)(2,1)S(1)}, u32[]{:S(2)}, u32[]{:S(2)}) collective-permute-start(bf16[128,3584]{1,0:T(8,128)(2,1)S(1)} %relay.5.refs_1_.refs_2_), channel_id=1, source_target_pairs={{0,16},{1,9},{2,18},{3,11},{4,20},{5,13},{6,22},{7,15},{8,24},{9,1... | collective-permute-start | bytes 2752520 | tf_op jit(solution)/shard_map/ppermute | solution.py:113
  21.4 7.1 %collective-permute-start.6 = (bf16[64,2048]{1,0:T(8,128)(2,1)S(1)}, bf16[64,2048]{1,0:T(8,128)(2,1)S(1)}, u32[]{:S(2)}, u32[]{:S(2)}) collective-permute-start(bf16[64,2048]{1,0:T(8,128)(2,1)S(1)} %relay.6.refs_4_), channel_id=1, source_target_pairs={{0,2},{1,3},{2,0},{3,1},{4,6},{5,7},{6,4},{7,5},{8,10},{9,11},{10,... | collective-permute-start | bytes 786440 | tf_op jit(solution)/shard_map/ppermute | solution.py:126
  24.1 4.4 %collective-permute-start.2 = (bf16[64,2048]{1,0:T(8,128)(2,1)S(1)}, bf16[64,2048]{1,0:T(8,128)(2,1)S(1)}, u32[]{:S(2)}, u32[]{:S(2)}) collective-permute-start(bf16[64,2048]{1,0:T(8,128)(2,1)S(1)} %relay.4.refs_1_.refs_2_), channel_id=1, source_target_pairs={{0,1},{1,0},{2,3},{3,2},{4,5},{5,4},{6,7},{7,6},{8,9},{9,8},{10,11... | collective-permute-start | bytes 786440 | tf_op jit(solution)/shard_map/ppermute | solution.py:130
  24.1 4.4 %collective-permute-start.5 = (bf16[64,2048]{1,0:T(8,128)(2,1)S(1)}, bf16[64,2048]{1,0:T(8,128)(2,1)S(1)}, u32[]{:S(2)}, u32[]{:S(2)}) collective-permute-start(bf16[64,2048]{1,0:T(8,128)(2,1)S(1)} %relay.6.refs_4_), channel_id=1, source_target_pairs={{0,1},{1,0},{2,3},{3,2},{4,5},{5,4},{6,7},{7,6},{8,9},{9,8},{10,11... | collective-permute-start | bytes 786440 | tf_op jit(solution)/shard_map/ppermute | solution.py:130
  28.5 1.5 %collective-permute-start.7 = (bf16[64,2048]{1,0:T(8,128)(2,1)S(1)}, bf16[64,2048]{1,0:T(8,128)(2,1)S(1)}, u32[]{:S(2)}, u32[]{:S(2)}) collective-permute-start(bf16[64,2048]{1,0:T(8,128)(2,1)S(1)} %collective-permute-done.6.refs_6_), channel_id=1, source_target_pairs={{0,1},{1,0},{2,3},{3,2},{4,5},{5,4},{6,7},{7,6},{8,9},{9,8},{10,11... | collective-permute-start | bytes 786440 | tf_op jit(solution)/shard_map/ppermute | solution.py:130
  33.0 17.2 %collective-permute-start.12 = (bf16[2064,128]{1,0:T(8,128)(2,1)S(1)}, bf16[2064,128]{1,0:T(8,128)(2,1)S(1)}, u32[]{:S(2)}, u32[]{:S(2)}) collective-permute-start(bf16[2064,128]{1,0:T(8,128)(2,1)S(1)} %get-tuple-element.32), channel_id=1, source_target_pairs={{0,8},{1,17},{2,10},{3,19},{4,12},{5,21},{6,14},{7,23},{8,0},{9,25... | collective-permute-start | bytes 1585160 | tf_op jit(solution)/shard_map/ppermute | solution.py:113
  38.1 13.2 %collective-permute-start.11 = (bf16[2064,128]{1,0:T(8,128)(2,1)S(1)}, bf16[2064,128]{1,0:T(8,128)(2,1)S(1)}, u32[]{:S(2)}, u32[]{:S(2)}) collective-permute-start(bf16[2064,128]{1,0:T(8,128)(2,1)S(1)} %relay.7), channel_id=1, source_target_pairs={{0,8},{1,17},{2,10},{3,19},{4,12},{5,21},{6,14},{7,23},{8,0},{9,25... | collective-permute-start | bytes 1585160 | tf_op jit(solution)/shard_map/ppermute | solution.py:113
  40.9 15.8 %collective-permute-start.8 = (bf16[2064,128]{1,0:T(8,128)(2,1)S(1)}, bf16[2064,128]{1,0:T(8,128)(2,1)S(1)}, u32[]{:S(2)}, u32[]{:S(2)}) collective-permute-start(bf16[2064,128]{1,0:T(8,128)(2,1)S(1)} %get-tuple-element.29), channel_id=1, source_target_pairs={{0,8},{1,17},{2,10},{3,19},{4,12},{5,21},{6,14},{7,23},{8,0},{9,25... | collective-permute-start | bytes 1585160 | tf_op jit(solution)/shard_map/ppermute | solution.py:113
  44.4 16.6 %collective-permute-start.14 = (bf16[1040,128]{1,0:T(8,128)(2,1)S(1)}, bf16[1040,128]{1,0:T(8,128)(2,1)S(1)}, u32[]{:S(2)}, u32[]{:S(2)}) collective-permute-start(bf16[1040,128]{1,0:T(8,128)(2,1)S(1)} %get-tuple-element.37), channel_id=1, source_target_pairs={{0,8},{1,17},{2,10},{3,19},{4,12},{5,21},{6,14},{7,23},{8,0},{9,25... | collective-permute-start | bytes 798728 | tf_op jit(solution)/shard_map/ppermute | solution.py:113
  50.5 11.7 %collective-permute-start.16 = (bf16[1040,128]{1,0:T(8,128)(2,1)S(1)}, bf16[1040,128]{1,0:T(8,128)(2,1)S(1)}, u32[]{:S(2)}, u32[]{:S(2)}) collective-permute-start(bf16[1040,128]{1,0:T(8,128)(2,1)S(1)} %combine.4.refs_2_), channel_id=1, source_target_pairs={{0,16},{1,9},{2,18},{3,11},{4,20},{5,13},{6,22},{7,15},{8,24},{9,1... | collective-permute-start | bytes 798728 | tf_op jit(solution)/shard_map/ppermute | solution.py:113
  51.6 10.6 %collective-permute-start.17 = (bf16[1040,128]{1,0:T(8,128)(2,1)S(1)}, bf16[1040,128]{1,0:T(8,128)(2,1)S(1)}, u32[]{:S(2)}, u32[]{:S(2)}) collective-permute-start(bf16[1040,128]{1,0:T(8,128)(2,1)S(1)} %combine.5.refs_4_), channel_id=1, source_target_pairs={{0,16},{1,9},{2,18},{3,11},{4,20},{5,13},{6,22},{7,15},{8,24},{9,1... | collective-permute-start | bytes 798728 | tf_op jit(solution)/shard_map/ppermute | solution.py:113
  57.0 9.4 %collective-permute-start.13 = (bf16[1040,128]{1,0:T(8,128)(2,1)S(1)}, bf16[1040,128]{1,0:T(8,128)(2,1)S(1)}, u32[]{:S(2)}, u32[]{:S(2)}) collective-permute-start(bf16[1040,128]{1,0:T(8,128)(2,1)S(1)} %combine.6.refs_2_), channel_id=1, source_target_pairs={{0,16},{1,9},{2,18},{3,11},{4,20},{5,13},{6,22},{7,15},{8,24},{9,1... | collective-permute-start | bytes 798728 | tf_op jit(solution)/shard_map/ppermute | solution.py:113
  61.2 5.2 %collective-permute-start.15 = (bf16[528,128]{1,0:T(8,128)(2,1)S(1)}, bf16[528,128]{1,0:T(8,128)(2,1)S(1)}, u32[]{:S(2)}, u32[]{:S(2)}) collective-permute-start(bf16[528,128]{1,0:T(8,128)(2,1)S(1)} %combine.7.refs_6_), channel_id=1, source_target_pairs={{0,16},{1,9},{2,18},{3,11},{4,20},{5,13},{6,22},{7,15},{8,24},{9,1... | collective-permute-start | bytes 405512 | tf_op jit(solution)/shard_map/ppermute | solution.py:113

commit v4 on v3

--- a/solution.py
+++ b/solution.py
@@ -336,9 +336,9 @@
     side = [plan.send_row(hidden, 0, s) for s in range(1, n2)]
     weight, swapped[0] = plan.stage(weight, swapped[0])
     far[1] = plan.relay([far[1]], [weight])[0]
+    later = [d for d in far if d > 1]
+    far.update(zip(later, plan.relay([far[d] for d in later], [far[1]])))
     near = plan.relay(near, [far[1]])
-    later = [d for d in far if d > 1]
-    far.update(zip(later, plan.relay([far[d] for d in later], near)))
     pieces = [out_grad] + swapped
     for d in range(1, plan.nz):
         if d not in far:
@@ -394,7 +394,7 @@
 
 
 ROUNDS = (4, 4, 4, 2)
-RUNS = (7, 4, 3)
+RUNS = (7, 6, 1)
 ENDS = 2
 WAIT = 1
 PROGRAM = [

time: 69.8 us -> 69.6 us (level)
  transfers between devices with their start and end apart: 18 -> 18, of which waited for: 5 -> 6; matrix products, arithmetic and copies ran while one was open for 0% -> 0% of each run, Pallas kernels for 45% -> 46%
where the time goes in v4:
time: 69.6 us; the launch traced here: 68.4 us
  Pallas kernels  33 us (47%)
  starting transfers between devices  22.1 us (32%)
  waiting for transfers between devices  12.3 us (18%)
  between operations  0.96 us (1%)
    pallas_call x20, Pallas kernels, call(): pl.pallas_call(kernel, in_specs=[pl.BlockSpec(memory_space=memory) for _,...  33 us
    ppermute x11, starting transfers between devices, send_row(): return lax.ppermute(array, ('row', 'col'), pairs)  14.7 us
    ppermute x3, starting transfers between devices, send_z(): return lax.ppermute(array, 'col', pairs)  6.87 us
    ppermute x3, waiting for transfers between devices, send_z(): return lax.ppermute(array, 'col', pairs)  6.07 us
    ppermute x11, waiting for transfers between devices, send_row(): return lax.ppermute(array, ('row', 'col'), pairs)  4.69 us
    ppermute x4, waiting for transfers between devices, swap(): return lax.ppermute(array, 'col', pairs)  1.53 us
  transfers between devices with their start and end apart: 18, of which 6 were waited for; matrix products, arithmetic and copies ran while one was open for 0% of the time, Pallas kernels for 46%

profile of v4, /device:TPU:0, one launch (start us, length us, event | category | flops | bytes accessed | tf_op | source)
XLA Modules:
  0.0 68.4 jit_solution(1722779772072245558)
XLA Ops:
  0.6 3.0 %collective-permute-start.9 = (bf16[128,3584]{1,0:T(8,128)(2,1)}, bf16[128,3584]{1,0:T(8,128)(2,1)S(1)}, u32[]{:S(2)}, u32[]{:S(2)}) collective-permute-start(bf16[128,3584]{1,0:T(8,128)(2,1)} %hidden_ref.1), channel_id=1, source_target_pairs={{0,8},{1,17},{2,10},{3,19},{4,12},{5,21},{6,14},{7,23},{8,0},{9,25... | collective-permute-start | bytes 2752520 | tf_op jit(solution)/shard_map/ppermute | solution.py:113
  3.6 0.0 collective-permute-start
  3.6 1.6 %collective-permute-start.1 = (bf16[64,2048]{1,0:T(8,128)(2,1)}, bf16[64,2048]{1,0:T(8,128)(2,1)S(1)}, u32[]{:S(2)}, u32[]{:S(2)}) collective-permute-start(bf16[64,2048]{1,0:T(8,128)(2,1)} %refs_0_.1), channel_id=1, source_target_pairs={{0,2},{1,3},{2,0},{3,1},{4,6},{5,7},{6,4},{7,5},{8,10},{9,11},{10,... | collective-permute-start | bytes 786440 | tf_op jit(solution)/shard_map/ppermute | solution.py:126
  5.2 2.6 %collective-permute-start.3 = (bf16[64,2048]{1,0:T(8,128)(2,1)}, bf16[64,2048]{1,0:T(8,128)(2,1)S(1)}, u32[]{:S(2)}, u32[]{:S(2)}) collective-permute-start(bf16[64,2048]{1,0:T(8,128)(2,1)} %refs_0_.1), channel_id=1, source_target_pairs={{0,4},{1,5},{2,6},{3,7},{4,0},{5,1},{6,2},{7,3},{8,12},{9,13},{10,... | collective-permute-start | bytes 786440 | tf_op jit(solution)/shard_map/ppermute | solution.py:126
  7.8 0.0 collective-permute-done.refs_0_
  7.8 1.2 %hold.1 = (bf16[128,3584]{1,0:T(8,128)(2,1)S(1)}, bf16[64,2048]{1,0:T(8,128)(2,1)S(1)}) custom-call(bf16[128,3584]{1,0:T(8,128)(2,1)} %hidden_ref.1, bf16[64,2048]{1,0:T(8,128)(2,1)S(1)} %collective-permute-done.refs_0_), custom_call_target="tpu_custom_call", output_to_operand_aliasing={{1}: (1, {})} | custom-call | tf_op jit(solution)/shard_map/hold/pallas_call | solution.py:24
  9.0 1.6 %collective-permute-start.8 = (bf16[128,3584]{1,0:T(8,128)(2,1)S(1)}, bf16[128,3584]{1,0:T(8,128)(2,1)S(1)}, u32[]{:S(2)}, u32[]{:S(2)}) collective-permute-start(bf16[128,3584]{1,0:T(8,128)(2,1)S(1)} %get-tuple-element.30.refs_0_), channel_id=1, source_target_pairs={{0,16},{1,9},{2,18},{3,11},{4,20},{5,13},{6,22},{7,15},{8,24},{9,1... | collective-permute-start | bytes 2752520 | tf_op jit(solution)/shard_map/ppermute | solution.py:113
  10.6 0.0 copy-start
  10.6 5.2 %stage.1 = (bf16[3584,2048]{1,0:T(8,128)(2,1)S(1)}, bf16[64,2048]{1,0:T(8,128)(2,1)S(1)}) custom-call(bf16[3584,2048]{1,0:T(8,128)(2,1)} %weight_ref.1, bf16[64,2048]{1,0:T(8,128)(2,1)S(1)} %get-tuple-element.23.refs_0_), custom_call_target="tpu_custom_call", output_to_operand_aliasing={{1}: (1, {})} | custom-call | tf_op jit(solution)/shard_map/stage/pallas_call | solution.py:24
  15.8 2.2 %collective-permute-done.1.refs_0_ = bf16[64,2048]{1,0:T(8,128)(2,1)S(1)} collective-permute-done((bf16[64,2048]{1,0:T(8,128)(2,1)}, bf16[64,2048]{1,0:T(8,128)(2,1)S(1)}, u32[]{:S(2)}, u32[]{:S(2)}) %collective-permute-start.1) | collective-permute-done | bytes 262176 | tf_op jit(solution)/shard_map/ppermute | solution.py:126
  18.1 1.8 %collective-permute-done.9.refs_0_ = bf16[128,3584]{1,0:T(8,128)(2,1)S(1)} collective-permute-done((bf16[128,3584]{1,0:T(8,128)(2,1)}, bf16[128,3584]{1,0:T(8,128)(2,1)S(1)}, u32[]{:S(2)}, u32[]{:S(2)}) %collective-permute-start.9) | collective-permute-done | bytes 917536 | tf_op jit(solution)/shard_map/ppermute | solution.py:113
  19.9 1.6 %collective-permute-start.10 = (bf16[128,3584]{1,0:T(8,128)(2,1)S(1)}, bf16[128,3584]{1,0:T(8,128)(2,1)S(1)}, u32[]{:S(2)}, u32[]{:S(2)}) collective-permute-start(bf16[128,3584]{1,0:T(8,128)(2,1)S(1)} %relay.6.refs_2_), channel_id=1, source_target_pairs={{0,16},{1,9},{2,18},{3,11},{4,20},{5,13},{6,22},{7,15},{8,24},{9,1... | collective-permute-start | bytes 2752520 | tf_op jit(solution)/shard_map/ppermute | solution.py:113
  21.4 0.0 collective-permute-done.3.refs_0_
  21.4 2.7 %collective-permute-start.5 = (bf16[64,2048]{1,0:T(8,128)(2,1)S(1)}, bf16[64,2048]{1,0:T(8,128)(2,1)S(1)}, u32[]{:S(2)}, u32[]{:S(2)}) collective-permute-start(bf16[64,2048]{1,0:T(8,128)(2,1)S(1)} %relay.5.refs_4_), channel_id=1, source_target_pairs={{0,2},{1,3},{2,0},{3,1},{4,6},{5,7},{6,4},{7,5},{8,10},{9,11},{10,... | collective-permute-start | bytes 786440 | tf_op jit(solution)/shard_map/ppermute | solution.py:126
  24.1 0.0 collective-permute-start.4
  24.1 0.5 collective-permute-start.2
  24.6 3.8 %collective-permute-done.5.refs_6_ = bf16[64,2048]{1,0:T(8,128)(2,1)S(1)} collective-permute-done((bf16[64,2048]{1,0:T(8,128)(2,1)S(1)}, bf16[64,2048]{1,0:T(8,128)(2,1)S(1)}, u32[]{:S(2)}, u32[]{:S(2)}) %collective-permute-start.5) | collective-permute-done | bytes 262176 | tf_op jit(solution)/shard_map/ppermute | solution.py:126
  28.5 0.0 collective-permute-start.6
  28.5 0.0 collective-permute-done.4.refs_5_
  28.5 0.0 collective-permute-done.2.refs_3_
  28.5 1.5 %collective-permute-done.6.refs_7_ = bf16[64,2048]{1,0:T(8,128)(2,1)S(1)} collective-permute-done((bf16[64,2048]{1,0:T(8,128)(2,1)S(1)}, bf16[64,2048]{1,0:T(8,128)(2,1)S(1)}, u32[]{:S(2)}, u32[]{:S(2)}) %collective-permute-start.6) | collective-permute-done | bytes 262176 | tf_op jit(solution)/shard_map/ppermute | solution.py:130
  30.0 0.0 copy-done
  30.0 0.3 gather_tokens.1.held_ref
  30.3 2.7 %token_part.4 = (bf16[2064,128]{1,0:T(8,128)(2,1)S(1)}, f32[256,1024]{1,0:T(8,128)S(1)}) custom-call(bf16[512,2048]{1,0:T(8,128)(2,1)S(1)} %gather_tokens.1.held_ref, bf16[3584,2048]{1,0:T(8,128)(2,1)S(1)} %get-tuple-element.25.refs_1_.weight_ref), custom_call_target="tpu_custom_call" | custom-call | flops 2000000000 | tf_op jit(solution)/shard_map/token_part/pallas_call | solution.py:24
  33.0 2.4 %collective-permute-start.12 = (bf16[2064,128]{1,0:T(8,128)(2,1)S(1)}, bf16[2064,128]{1,0:T(8,128)(2,1)S(1)}, u32[]{:S(2)}, u32[]{:S(2)}) collective-permute-start(bf16[2064,128]{1,0:T(8,128)(2,1)S(1)} %get-tuple-element.32), channel_id=1, source_target_pairs={{0,8},{1,17},{2,10},{3,19},{4,12},{5,21},{6,14},{7,23},{8,0},{9,25... | collective-permute-start | bytes 1585160 | tf_op jit(solution)/shard_map/ppermute | solution.py:113
  35.4 2.7 %token_part.5 = (bf16[2064,128]{1,0:T(8,128)(2,1)S(1)}, f32[256,1024]{1,0:T(8,128)S(1)}) custom-call(bf16[512,2048]{1,0:T(8,128)(2,1)S(1)} %gather_tokens.1.held_ref, bf16[3584,2048]{1,0:T(8,128)(2,1)S(1)} %get-tuple-element.25.refs_1_.weight_ref, f32[256,1024]{1,0:T(8,128)S(1)} %get-tuple-element.26.refs_0_.refs_1_), custom_call_target="tpu_custom_call" | custom-call | flops 2000000000 | tf_op jit(solution)/shard_map/token_part/pallas_call | solution.py:24
  38.1 0.0 collective-permute-done.8.refs_2_.refs_1_
  38.1 0.0 collective-permute-done.10.refs_1_.refs_3_
  38.1 0.1 collective-permute-start.11
  38.2 2.7 %token_part.6 = (bf16[2064,128]{1,0:T(8,128)(2,1)S(1)}, f32[256,1024]{1,0:T(8,128)S(1)}) custom-call(bf16[512,2048]{1,0:T(8,128)(2,1)S(1)} %gather_tokens.1.held_ref, bf16[3584,2048]{1,0:T(8,128)(2,1)S(1)} %get-tuple-element.25.refs_1_.weight_ref, f32[256,1024]{1,0:T(8,128)S(1)} %get-tuple-element.27.refs_0_.refs_1_.refs_3_), custom_call_target="tpu_custom_call" | custom-call | tf_op jit(solution)/shard_map/token_part/pallas_call | solution.py:24
  40.9 2.1 %collective-permute-start.7 = (bf16[2064,128]{1,0:T(8,128)(2,1)S(1)}, bf16[2064,128]{1,0:T(8,128)(2,1)S(1)}, u32[]{:S(2)}, u32[]{:S(2)}) collective-permute-start(bf16[2064,128]{1,0:T(8,128)(2,1)S(1)} %get-tuple-element.29), channel_id=1, source_target_pairs={{0,8},{1,17},{2,10},{3,19},{4,12},{5,21},{6,14},{7,23},{8,0},{9,25... | collective-permute-start | bytes 1585160 | tf_op jit(solution)/shard_map/ppermute | solution.py:113
  42.9 1.4 %token_part.7 = (bf16[1040,128]{1,0:T(8,128)(2,1)S(1)}, f32[256,512]{1,0:T(8,128)S(1)}) custom-call(bf16[512,2048]{1,0:T(8,128)(2,1)S(1)} %gather_tokens.1.held_ref, bf16[3584,2048]{1,0:T(8,128)(2,1)S(1)} %get-tuple-element.25.refs_1_.weight_ref, f32[256,1024]{1,0:T(8,128)S(1)} %get-tuple-element.28.refs_0_.refs_1_), custom_call_target="tpu_custom_call" | custom-call | tf_op jit(solution)/shard_map/token_part/pallas_call | solution.py:24
  44.4 0.1 collective-permute-start.14
  44.5 5.7 %weight_part.3 = (bf16[3584,2048]{1,0:T(8,128)(2,1)}, f32[8,128]{1,0:T(8,128)S(1)}) custom-call(bf16[512,2048]{1,0:T(8,128)(2,1)S(1)} %gather_tokens.1.held_ref, bf16[128,3584]{1,0:T(8,128)(2,1)S(1)} %get-tuple-element.30.refs_0_, bf16[128,3584]{1,0:T(8,128)(2,1)S(1)} %collective-permute-done.8.refs_2_.refs_1_, bf16[128,3584]{1,0:T(8,128)(2,1)S(1)} %relay.6.refs_2_, ...), custom_call_target="tpu_custom_call" | custom-call | tf_op jit(solution)/shard_map/weight_part/pallas_call | solution.py:24
  50.1 0.0 collective-permute-done.12.refs_0_.refs_1_
  50.1 0.4 combine.4.refs_2_
  50.5 0.8 %collective-permute-start.16 = (bf16[1040,128]{1,0:T(8,128)(2,1)S(1)}, bf16[1040,128]{1,0:T(8,128)(2,1)S(1)}, u32[]{:S(2)}, u32[]{:S(2)}) collective-permute-start(bf16[1040,128]{1,0:T(8,128)(2,1)S(1)} %combine.4.refs_2_), channel_id=1, source_target_pairs={{0,16},{1,9},{2,18},{3,11},{4,20},{5,13},{6,22},{7,15},{8,24},{9,1... | collective-permute-start | bytes 798728 | tf_op jit(solution)/shard_map/ppermute | solution.py:113
  51.3 0.0 collective-permute-done.11.refs_0_.refs_4_
  51.3 0.4 combine.5.refs_4_
  51.6 1.4 %collective-permute-start.17 = (bf16[1040,128]{1,0:T(8,128)(2,1)S(1)}, bf16[1040,128]{1,0:T(8,128)(2,1)S(1)}, u32[]{:S(2)}, u32[]{:S(2)}) collective-permute-start(bf16[1040,128]{1,0:T(8,128)(2,1)S(1)} %combine.5.refs_4_), channel_id=1, source_target_pairs={{0,16},{1,9},{2,18},{3,11},{4,20},{5,13},{6,22},{7,15},{8,24},{9,1... | collective-permute-start | bytes 798728 | tf_op jit(solution)/shard_map/ppermute | solution.py:113
  53.0 5.1 %weight_part.4 = (bf16[3584,2048]{1,0:T(8,128)(2,1)}, f32[8,128]{1,0:T(8,128)S(1)}) custom-call(bf16[512,2048]{1,0:T(8,128)(2,1)S(1)} %gather_tokens.1.held_ref, bf16[128,3584]{1,0:T(8,128)(2,1)S(1)} %get-tuple-element.30.refs_0_, bf16[128,3584]{1,0:T(8,128)(2,1)S(1)} %collective-permute-done.8.refs_2_.refs_1_, ...), custom_call_target="tpu_custom_call", output_to_operand_aliasing={{0}: (6, {})} | custom-call | tf_op jit(solution)/shard_map/weight_part/pallas_call | solution.py:24
  58.1 0.0 collective-permute-done.7.refs_0_.refs_1_
  58.1 0.4 combine.6.refs_2_
  58.5 0.8 %collective-permute-start.13 = (bf16[1040,128]{1,0:T(8,128)(2,1)S(1)}, bf16[1040,128]{1,0:T(8,128)(2,1)S(1)}, u32[]{:S(2)}, u32[]{:S(2)}) collective-permute-start(bf16[1040,128]{1,0:T(8,128)(2,1)S(1)} %combine.6.refs_2_), channel_id=1, source_target_pairs={{0,16},{1,9},{2,18},{3,11},{4,20},{5,13},{6,22},{7,15},{8,24},{9,1... | collective-permute-start | bytes 798728 | tf_op jit(solution)/shard_map/ppermute | solution.py:113
  59.2 1.8 %collective-permute-done.14.refs_0_.refs_4_ = bf16[1040,128]{1,0:T(8,128)(2,1)S(1)} collective-permute-done((bf16[1040,128]{1,0:T(8,128)(2,1)S(1)}, bf16[1040,128]{1,0:T(8,128)(2,1)S(1)}, u32[]{:S(2)}, u32[]{:S(2)}) %collective-permute-start.14) | collective-permute-done | bytes 266272 | tf_op jit(solution)/shard_map/ppermute | solution.py:113
  61.0 0.2 combine.7.refs_6_
  61.2 1.0 %collective-permute-start.15 = (bf16[528,128]{1,0:T(8,128)(2,1)S(1)}, bf16[528,128]{1,0:T(8,128)(2,1)S(1)}, u32[]{:S(2)}, u32[]{:S(2)}) collective-permute-start(bf16[528,128]{1,0:T(8,128)(2,1)S(1)} %combine.7.refs_6_), channel_id=1, source_target_pairs={{0,16},{1,9},{2,18},{3,11},{4,20},{5,13},{6,22},{7,15},{8,24},{9,1... | collective-permute-start | bytes 405512 | tf_op jit(solution)/shard_map/ppermute | solution.py:113
  62.2 0.0 collective-permute-done.16.refs_2_
  62.2 0.0 collective-permute-done.17.refs_5_
  62.2 1.4 %finish.2 = (bf16[128,3584]{1,0:T(8,128)(2,1)}, f32[8,128]{1,0:T(8,128)S(1)}) custom-call(f32[256,1024]{1,0:T(8,128)S(1)} %get-tuple-element.26.refs_0_.refs_1_, bf16[2064,128]{1,0:T(8,128)(2,1)S(1)} %collective-permute-done.12.refs_0_.refs_1_, bf16[1040,128]{1,0:T(8,128)(2,1)S(1)} %collective-permute-done.16.refs_2_, ...), custom_call_target="tpu_custom_call" | custom-call | tf_op jit(solution)/shard_map/finish/pallas_call | solution.py:24
  63.6 1.8 %weight_part.5 = (bf16[3584,2048]{1,0:T(8,128)(2,1)}, f32[8,128]{1,0:T(8,128)S(1)}) custom-call(bf16[512,2048]{1,0:T(8,128)(2,1)S(1)} %gather_tokens.1.held_ref, bf16[128,3584]{1,0:T(8,128)(2,1)S(1)} %get-tuple-element.30.refs_0_, bf16[128,3584]{1,0:T(8,128)(2,1)S(1)} %collective-permute-done.8.refs_2_.refs_1_, ...), custom_call_target="tpu_custom_call", output_to_operand_aliasing={{0}: (6, {})} | custom-call | tf_op jit(solution)/shard_map/weight_part/pallas_call | solution.py:24
  65.3 1.1 %collective-permute-done.15.refs_5_ = bf16[528,128]{1,0:T(8,128)(2,1)S(1)} collective-permute-done((bf16[528,128]{1,0:T(8,128)(2,1)S(1)}, bf16[528,128]{1,0:T(8,128)(2,1)S(1)}, u32[]{:S(2)}, u32[]{:S(2)}) %collective-permute-start.15) | collective-permute-done | bytes 135200 | tf_op jit(solution)/shard_map/ppermute | solution.py:113
  66.4 0.0 collective-permute-done.13.refs_2_
  66.4 1.8 %finish.3 = (bf16[128,3584]{1,0:T(8,128)(2,1)}, f32[8,128]{1,0:T(8,128)}) custom-call(f32[256,1024]{1,0:T(8,128)S(1)} %get-tuple-element.28.refs_0_.refs_1_, bf16[2064,128]{1,0:T(8,128)(2,1)S(1)} %collective-permute-done.7.refs_0_.refs_1_, bf16[1040,128]{1,0:T(8,128)(2,1)S(1)} %collective-permute-done.13.refs_2_, ...), custom_call_target="tpu_custom_call", output_to_operand_aliasing={{0}: (7, {})} | custom-call | tf_op jit(solution)/shard_map/finish/pallas_call | solution.py:24
  (4 shorter events, 0.0 us)
Async XLA Ops:
  0.6 19.2 %collective-permute-start.9 = (bf16[128,3584]{1,0:T(8,128)(2,1)}, bf16[128,3584]{1,0:T(8,128)(2,1)S(1)}, u32[]{:S(2)}, u32[]{:S(2)}) collective-permute-start(bf16[128,3584]{1,0:T(8,128)(2,1)} %hidden_ref.1), channel_id=1, source_target_pairs={{0,8},{1,17},{2,10},{3,19},{4,12},{5,21},{6,14},{7,23},{8,0},{9,25... | collective-permute-start | bytes 2752520 | tf_op jit(solution)/shard_map/ppermute | solution.py:113
  3.6 4.2 %collective-permute-start = (bf16[64,2048]{1,0:T(8,128)(2,1)}, bf16[64,2048]{1,0:T(8,128)(2,1)S(1)}, u32[]{:S(2)}, u32[]{:S(2)}) collective-permute-start(bf16[64,2048]{1,0:T(8,128)(2,1)} %refs_0_.1), channel_id=1, source_target_pairs={{0,1},{1,0},{2,3},{3,2},{4,5},{5,4},{6,7},{7,6},{8,9},{9,8},{10,11... | collective-permute-start | bytes 786440 | tf_op jit(solution)/shard_map/ppermute | solution.py:130
  3.6 14.4 %collective-permute-start.1 = (bf16[64,2048]{1,0:T(8,128)(2,1)}, bf16[64,2048]{1,0:T(8,128)(2,1)S(1)}, u32[]{:S(2)}, u32[]{:S(2)}) collective-permute-start(bf16[64,2048]{1,0:T(8,128)(2,1)} %refs_0_.1), channel_id=1, source_target_pairs={{0,2},{1,3},{2,0},{3,1},{4,6},{5,7},{6,4},{7,5},{8,10},{9,11},{10,... | collective-permute-start | bytes 786440 | tf_op jit(solution)/shard_map/ppermute | solution.py:126
  5.2 16.2 %collective-permute-start.3 = (bf16[64,2048]{1,0:T(8,128)(2,1)}, bf16[64,2048]{1,0:T(8,128)(2,1)S(1)}, u32[]{:S(2)}, u32[]{:S(2)}) collective-permute-start(bf16[64,2048]{1,0:T(8,128)(2,1)} %refs_0_.1), channel_id=1, source_target_pairs={{0,4},{1,5},{2,6},{3,7},{4,0},{5,1},{6,2},{7,3},{8,12},{9,13},{10,... | collective-permute-start | bytes 786440 | tf_op jit(solution)/shard_map/ppermute | solution.py:126
  9.0 29.1 %collective-permute-start.8 = (bf16[128,3584]{1,0:T(8,128)(2,1)S(1)}, bf16[128,3584]{1,0:T(8,128)(2,1)S(1)}, u32[]{:S(2)}, u32[]{:S(2)}) collective-permute-start(bf16[128,3584]{1,0:T(8,128)(2,1)S(1)} %get-tuple-element.30.refs_0_), channel_id=1, source_target_pairs={{0,16},{1,9},{2,18},{3,11},{4,20},{5,13},{6,22},{7,15},{8,24},{9,1... | collective-permute-start | bytes 2752520 | tf_op jit(solution)/shard_map/ppermute | solution.py:113
  10.6 19.4 %copy-start = (bf16[64,2048]{1,0:T(8,128)(2,1)S(1)}, bf16[64,2048]{1,0:T(8,128)(2,1)}, u32[]{:S(2)}) copy-start(bf16[64,2048]{1,0:T(8,128)(2,1)} %refs_0_.1) | copy-start | bytes 786436
  19.9 18.2 %collective-permute-start.10 = (bf16[128,3584]{1,0:T(8,128)(2,1)S(1)}, bf16[128,3584]{1,0:T(8,128)(2,1)S(1)}, u32[]{:S(2)}, u32[]{:S(2)}) collective-permute-start(bf16[128,3584]{1,0:T(8,128)(2,1)S(1)} %relay.6.refs_2_), channel_id=1, source_target_pairs={{0,16},{1,9},{2,18},{3,11},{4,20},{5,13},{6,22},{7,15},{8,24},{9,1... | collective-permute-start | bytes 2752520 | tf_op jit(solution)/shard_map/ppermute | solution.py:113
  21.4 7.1 %collective-permute-start.5 = (bf16[64,2048]{1,0:T(8,128)(2,1)S(1)}, bf16[64,2048]{1,0:T(8,128)(2,1)S(1)}, u32[]{:S(2)}, u32[]{:S(2)}) collective-permute-start(bf16[64,2048]{1,0:T(8,128)(2,1)S(1)} %relay.5.refs_4_), channel_id=1, source_target_pairs={{0,2},{1,3},{2,0},{3,1},{4,6},{5,7},{6,4},{7,5},{8,10},{9,11},{10,... | collective-permute-start | bytes 786440 | tf_op jit(solution)/shard_map/ppermute | solution.py:126
  24.1 4.4 %collective-permute-start.4 = (bf16[64,2048]{1,0:T(8,128)(2,1)S(1)}, bf16[64,2048]{1,0:T(8,128)(2,1)S(1)}, u32[]{:S(2)}, u32[]{:S(2)}) collective-permute-start(bf16[64,2048]{1,0:T(8,128)(2,1)S(1)} %relay.5.refs_4_), channel_id=1, source_target_pairs={{0,1},{1,0},{2,3},{3,2},{4,5},{5,4},{6,7},{7,6},{8,9},{9,8},{10,11... | collective-permute-start | bytes 786440 | tf_op jit(solution)/shard_map/ppermute | solution.py:130
  24.1 4.4 %collective-permute-start.2 = (bf16[64,2048]{1,0:T(8,128)(2,1)S(1)}, bf16[64,2048]{1,0:T(8,128)(2,1)S(1)}, u32[]{:S(2)}, u32[]{:S(2)}) collective-permute-start(bf16[64,2048]{1,0:T(8,128)(2,1)S(1)} %relay.4.refs_1_.refs_2_), channel_id=1, source_target_pairs={{0,1},{1,0},{2,3},{3,2},{4,5},{5,4},{6,7},{7,6},{8,9},{9,8},{10,11... | collective-permute-start | bytes 786440 | tf_op jit(solution)/shard_map/ppermute | solution.py:130
  28.5 1.5 %collective-permute-start.6 = (bf16[64,2048]{1,0:T(8,128)(2,1)S(1)}, bf16[64,2048]{1,0:T(8,128)(2,1)S(1)}, u32[]{:S(2)}, u32[]{:S(2)}) collective-permute-start(bf16[64,2048]{1,0:T(8,128)(2,1)S(1)} %collective-permute-done.5.refs_6_), channel_id=1, source_target_pairs={{0,1},{1,0},{2,3},{3,2},{4,5},{5,4},{6,7},{7,6},{8,9},{9,8},{10,11... | collective-permute-start | bytes 786440 | tf_op jit(solution)/shard_map/ppermute | solution.py:130
  33.0 17.2 %collective-permute-start.12 = (bf16[2064,128]{1,0:T(8,128)(2,1)S(1)}, bf16[2064,128]{1,0:T(8,128)(2,1)S(1)}, u32[]{:S(2)}, u32[]{:S(2)}) collective-permute-start(bf16[2064,128]{1,0:T(8,128)(2,1)S(1)} %get-tuple-element.32), channel_id=1, source_target_pairs={{0,8},{1,17},{2,10},{3,19},{4,12},{5,21},{6,14},{7,23},{8,0},{9,25... | collective-permute-start | bytes 1585160 | tf_op jit(solution)/shard_map/ppermute | solution.py:113
  38.1 13.2 %collective-permute-start.11 = (bf16[2064,128]{1,0:T(8,128)(2,1)S(1)}, bf16[2064,128]{1,0:T(8,128)(2,1)S(1)}, u32[]{:S(2)}, u32[]{:S(2)}) collective-permute-start(bf16[2064,128]{1,0:T(8,128)(2,1)S(1)} %relay.7), channel_id=1, source_target_pairs={{0,8},{1,17},{2,10},{3,19},{4,12},{5,21},{6,14},{7,23},{8,0},{9,25... | collective-permute-start | bytes 1585160 | tf_op jit(solution)/shard_map/ppermute | solution.py:113
  40.9 17.3 %collective-permute-start.7 = (bf16[2064,128]{1,0:T(8,128)(2,1)S(1)}, bf16[2064,128]{1,0:T(8,128)(2,1)S(1)}, u32[]{:S(2)}, u32[]{:S(2)}) collective-permute-start(bf16[2064,128]{1,0:T(8,128)(2,1)S(1)} %get-tuple-element.29), channel_id=1, source_target_pairs={{0,8},{1,17},{2,10},{3,19},{4,12},{5,21},{6,14},{7,23},{8,0},{9,25... | collective-permute-start | bytes 1585160 | tf_op jit(solution)/shard_map/ppermute | solution.py:113
  44.4 16.6 %collective-permute-start.14 = (bf16[1040,128]{1,0:T(8,128)(2,1)S(1)}, bf16[1040,128]{1,0:T(8,128)(2,1)S(1)}, u32[]{:S(2)}, u32[]{:S(2)}) collective-permute-start(bf16[1040,128]{1,0:T(8,128)(2,1)S(1)} %get-tuple-element.37), channel_id=1, source_target_pairs={{0,8},{1,17},{2,10},{3,19},{4,12},{5,21},{6,14},{7,23},{8,0},{9,25... | collective-permute-start | bytes 798728 | tf_op jit(solution)/shard_map/ppermute | solution.py:113
  50.5 11.7 %collective-permute-start.16 = (bf16[1040,128]{1,0:T(8,128)(2,1)S(1)}, bf16[1040,128]{1,0:T(8,128)(2,1)S(1)}, u32[]{:S(2)}, u32[]{:S(2)}) collective-permute-start(bf16[1040,128]{1,0:T(8,128)(2,1)S(1)} %combine.4.refs_2_), channel_id=1, source_target_pairs={{0,16},{1,9},{2,18},{3,11},{4,20},{5,13},{6,22},{7,15},{8,24},{9,1... | collective-permute-start | bytes 798728 | tf_op jit(solution)/shard_map/ppermute | solution.py:113
  51.6 10.6 %collective-permute-start.17 = (bf16[1040,128]{1,0:T(8,128)(2,1)S(1)}, bf16[1040,128]{1,0:T(8,128)(2,1)S(1)}, u32[]{:S(2)}, u32[]{:S(2)}) collective-permute-start(bf16[1040,128]{1,0:T(8,128)(2,1)S(1)} %combine.5.refs_4_), channel_id=1, source_target_pairs={{0,16},{1,9},{2,18},{3,11},{4,20},{5,13},{6,22},{7,15},{8,24},{9,1... | collective-permute-start | bytes 798728 | tf_op jit(solution)/shard_map/ppermute | solution.py:113
  58.5 7.9 %collective-permute-start.13 = (bf16[1040,128]{1,0:T(8,128)(2,1)S(1)}, bf16[1040,128]{1,0:T(8,128)(2,1)S(1)}, u32[]{:S(2)}, u32[]{:S(2)}) collective-permute-start(bf16[1040,128]{1,0:T(8,128)(2,1)S(1)} %combine.6.refs_2_), channel_id=1, source_target_pairs={{0,16},{1,9},{2,18},{3,11},{4,20},{5,13},{6,22},{7,15},{8,24},{9,1... | collective-permute-start | bytes 798728 | tf_op jit(solution)/shard_map/ppermute | solution.py:113
  61.2 5.2 %collective-permute-start.15 = (bf16[528,128]{1,0:T(8,128)(2,1)S(1)}, bf16[528,128]{1,0:T(8,128)(2,1)S(1)}, u32[]{:S(2)}, u32[]{:S(2)}) collective-permute-start(bf16[528,128]{1,0:T(8,128)(2,1)S(1)} %combine.7.refs_6_), channel_id=1, source_target_pairs={{0,16},{1,9},{2,18},{3,11},{4,20},{5,13},{6,22},{7,15},{8,24},{9,1... | collective-permute-start | bytes 405512 | tf_op jit(solution)/shard_map/ppermute | solution.py:113
